TPU v7x, 256 devices: a whole 4x4x8 slice. The times are simulated.
256 devices in a mesh: gx: 4 (over x), gy: 8 (over y, z_lo), gz: 8 (over z_hi, core).
Axes of the slice: x: 4, y: 4, z: 8 (z_hi: 4, z_lo: 2; z = z_hi * 2 + z_lo), core: 2. Of those that a mesh axis runs over, the one named last changes fastest.
Arguments:
- acts: bfloat16 [2048, 14336], P(('gz', 'gy'), 'gx'), may hold values from -6 to 6
- preact: bfloat16 [2048, 7168], P(('gz', 'gx'), 'gy'), may hold values from -6 to 6
- out_grad: bfloat16 [2048, 14336], P(('gz', 'gy'), 'gx'), may hold values from -2 to 2
- w_in: bfloat16 [14336, 7168], P(('gx', 'gz'), 'gy'), may hold values from -0.046875 to 0.046875
- w_out: bfloat16 [14336, 7168], P(('gx', 'gz'), 'gy'), may hold values from -0.0625 to 0.0625
Outputs:
- input_grad: bfloat16 [2048, 14336], P(('gz', 'gy'), 'gx')
- in_weight_grad: bfloat16 [14336, 7168], P(('gx', 'gz'), 'gy')
- out_weight_grad: bfloat16 [14336, 7168], P(('gx', 'gz'), 'gy')
- bias_grad: float32 [7168], P('gy')
All inputs are finite; a program needn't handle non-finite values.
Results may differ from a plain program's by a relative error of at most 0.025.
Values may be sent and summed in bfloat16 or wider, within the bound.
A program may use at most 128 MiB of HBM per device.

v0:
```python
import jax
import jax.numpy as jnp
from jax import lax
from jax.sharding import PartitionSpec as P


def gelu_parts(pre):
    coeff = 0.7978845608028654
    inner = coeff * (pre + 0.044715 * pre * pre * pre)
    tangent = jnp.tanh(inner)
    value = 0.5 * pre * (1.0 + tangent)
    slope = 0.5 * (1.0 + tangent) + 0.5 * pre * (1.0 - tangent * tangent) * coeff * (
        1.0 + 3.0 * 0.044715 * pre * pre
    )
    return (value, slope)


def left_product(left, right):
    return lax.dot_general(
        left, right, (((0,), (0,)), ((), ())), preferred_element_type=jnp.float32
    )


def right_product(left, right):
    return lax.dot_general(
        left, right, (((1,), (1,)), ((), ())), preferred_element_type=jnp.float32
    )


def shards(acts, preact, out_grad, w_in, w_out):
    acts_rows, grad_rows = (
        lax.all_gather(acts, "gy", axis=0, tiled=True),
        lax.all_gather(out_grad, "gy", axis=0, tiled=True),
    )
    columns = grad_rows
    partial_hidden = jnp.dot(
        columns, lax.all_gather(w_out, "gz", axis=0, tiled=True), preferred_element_type=jnp.float32
    )
    hidden_grad = lax.psum_scatter(
        partial_hidden.astype(jnp.bfloat16), "gx", scatter_dimension=0, tiled=True
    ).astype(jnp.float32)
    value, slope = gelu_parts(preact.astype(jnp.float32))
    act_local = value.astype(jnp.bfloat16)
    dh_local = (hidden_grad * slope).astype(jnp.bfloat16)
    act_rows, dh_rows = (
        lax.all_gather(act_local, "gx", axis=0, tiled=True),
        lax.all_gather(dh_local, "gx", axis=0, tiled=True),
    )
    bias_grad = lax.psum(jnp.sum(dh_rows.astype(jnp.float32), axis=0), "gz")
    columns = grad_rows
    out_weight_grad = lax.psum_scatter(
        left_product(columns, act_rows).astype(jnp.bfloat16), "gz", scatter_dimension=0, tiled=True
    )
    columns = acts_rows
    in_weight_grad = lax.psum_scatter(
        left_product(columns, dh_rows).astype(jnp.bfloat16), "gz", scatter_dimension=0, tiled=True
    )
    partial_input = right_product(dh_rows, lax.all_gather(w_in, "gz", axis=0, tiled=True)).astype(
        jnp.bfloat16
    )
    input_grad = lax.psum_scatter(
        partial_input.astype(jnp.float32).astype(jnp.bfloat16),
        "gy",
        scatter_dimension=0,
        tiled=True,
    )
    return (input_grad, in_weight_grad, out_weight_grad, bias_grad)


def solution(mesh):
    return jax.shard_map(
        shards,
        mesh=mesh,
        in_specs=(
            P(("gz", "gy"), "gx"),
            P(("gz", "gx"), "gy"),
            P(("gz", "gy"), "gx"),
            P(("gx", "gz"), "gy"),
            P(("gx", "gz"), "gy"),
        ),
        out_specs=(P(("gz", "gy"), "gx"), P(("gx", "gz"), "gy"), P(("gx", "gz"), "gy"), P("gy")),
        check_vma=False,
    )
```

profile of v0, /device:TPU:32, one launch (start us, length us, event | category | flops | bytes accessed | tf_op | source)
XLA Modules:
  0.0 508.5 jit_solution(1349956526128128998)
XLA Ops:
  7.2 0.0 all-gather.5.cloned.1.call-start
  7.2 0.7 all-gather.5.cloned.1.call-update
  7.9 0.0 all-gather.7.cloned.1.call-start
  7.9 0.7 all-gather.7.cloned.1.call-update
  8.6 0.0 copy-start.1
  8.7 0.0 reduce-scatter.9.cloned.1.call-start
  8.7 51.7 %all-gather.5.cloned.1.call-done = bf16[256,3584]{1,0:T(8,128)(2,1)} async-done(((bf16[32,3584]{1,0:T(8,128)(2,1)}), bf16[256,3584]{1,0:T(8,128)(2,1)}) %all-gather.5.cloned.1.call-update) | async-done | bytes 1835024 | tf_op jit(solution)/shard_map/all_gather | solution.py:33
  60.4 74.2 %all-gather.7.cloned.1.call-done = bf16[3584,896]{1,0:T(8,128)(2,1)} async-done(((bf16[448,896]{1,0:T(8,128)(2,1)}), bf16[3584,896]{1,0:T(8,128)(2,1)}) %all-gather.7.cloned.1.call-update) | async-done | bytes 6422544 | tf_op jit(solution)/shard_map/all_gather | solution.py:37
  134.5 6.2 %convolution_convert_fusion.3 = bf16[256,896]{1,0:T(8,128)(2,1)} fusion(bf16[256,3584]{1,0:T(8,128)(2,1)} %all-gather.5.cloned.1.call-done, bf16[3584,896]{1,0:T(8,128)(2,1)} %all-gather.7.cloned.1.call-done), kind=kOutput, calls=%fused_computation.5 | convolution fusion | flops 1644396544 | bytes 8716288 | tf_op jit(solution)/shard_map/dot_general | solution.py:36
  140.8 0.0 reduce-scatter.9.cloned.1.call-update
  140.8 0.0 all-gather.9.cloned.1.call-start
  140.8 0.5 all-gather.9.cloned.1.call-update
  141.4 0.0 all-gather.11.cloned.1.call-start
  141.4 0.5 all-gather.11.cloned.1.call-update
  141.9 0.0 reduce-scatter.11.cloned.1.call-start
  142.0 21.1 %reduce-scatter.9.cloned.1.call-done = bf16[64,896]{1,0:T(8,128)(2,1)} async-done(((bf16[256,896]{1,0:T(8,128)(2,1)}), bf16[64,896]{1,0:T(8,128)(2,1)}) %reduce-scatter.9.cloned.1.call-update) | async-done | bytes 114704 | tf_op jit(solution)/shard_map/reduce_scatter | solution.py:39
  163.1 0.0 copy-done.1
  163.1 1.1 fusion.9
  164.2 12.7 %all_gather.20 = bf16[256,896]{1,0:T(8,128)(2,1)S(1)} all-gather(bf16[64,896]{1,0:T(8,128)(2,1)S(1)} %get-tuple-element.13), channel_id=1, replica_groups=mesh['gx'=4,'gy'=8,'gz'=8] {'gx'}, dimensions={0}, use_global_device_ids=true | all-gather | bytes 573440 | tf_op jit(solution)/shard_map/all_gather | solution.py:47
  176.9 59.1 %all-gather.9.cloned.1.call-done = bf16[3584,896]{1,0:T(8,128)(2,1)} async-done(((bf16[448,896]{1,0:T(8,128)(2,1)}), bf16[3584,896]{1,0:T(8,128)(2,1)}) %all-gather.9.cloned.1.call-update) | async-done | bytes 6422544 | tf_op jit(solution)/shard_map/all_gather | solution.py:58
  235.9 6.2 %convolution_convert_fusion.2 = bf16[256,3584]{1,0:T(8,128)(2,1)} fusion(bf16[256,896]{1,0:T(8,128)(2,1)S(1)} %all_gather.20, bf16[3584,896]{1,0:T(8,128)(2,1)} %all-gather.9.cloned.1.call-done), kind=kOutput, calls=%fused_computation.4 | convolution fusion | flops 1645084672 | bytes 8716288 | tf_op jit(solution)/shard_map/dot_general | solution.py:25
  242.1 0.0 reduce-scatter.11.cloned.1.call-update
  242.1 0.0 reduce-scatter.13.cloned.1.call-start
  242.2 42.0 %all-gather.11.cloned.1.call-done = bf16[256,3584]{1,0:T(8,128)(2,1)} async-done(((bf16[32,3584]{1,0:T(8,128)(2,1)}), bf16[256,3584]{1,0:T(8,128)(2,1)}) %all-gather.11.cloned.1.call-update) | async-done | bytes 1835024 | tf_op jit(solution)/shard_map/all_gather | solution.py:32
  284.2 6.0 %fusion = bf16[3584,896]{0,1:T(8,128)(2,1)} fusion(bf16[256,896]{1,0:T(8,128)(2,1)S(1)} %all_gather.20, bf16[256,3584]{1,0:T(8,128)(2,1)} %all-gather.11.cloned.1.call-done), kind=kOutput, calls=%fused_computation.2 | convolution fusion | flops 1647378432 | bytes 8716288 | tf_op jit(solution)/shard_map/dot_general | solution.py:19
  290.2 9.6 %copy.13 = bf16[3584,896]{1,0:T(8,128)(2,1)} copy(bf16[3584,896]{0,1:T(8,128)(2,1)} %fusion) | data formatting | bytes 12845056
  299.8 0.0 copy-start
  299.8 0.0 reduce-scatter.13.cloned.1.call-update
  299.8 0.0 reduce-scatter.15.cloned.1.call-start
  299.8 13.1 %all_gather.23 = bf16[256,896]{1,0:T(8,128)(2,1)S(1)} all-gather(bf16[64,896]{1,0:T(8,128)(2,1)S(1)} %get-tuple-element.12), channel_id=1, replica_groups=mesh['gx'=4,'gy'=8,'gz'=8] {'gx'}, dimensions={0}, use_global_device_ids=true | all-gather | bytes 573440 | tf_op jit(solution)/shard_map/all_gather | solution.py:46
  312.9 0.0 copy-done
  312.9 4.5 fusion.1
  317.5 9.5 %copy.15 = bf16[3584,896]{1,0:T(8,128)(2,1)} copy(bf16[3584,896]{0,1:T(8,128)(2,1)} %fusion.1) | data formatting | bytes 12845056
  327.0 0.0 reduce-scatter.15.cloned.1.call-update
  327.0 0.1 convert_reduce_fusion
  327.1 16.9 %psum.7 = f32[896]{0:T(1024)} all-reduce(f32[896]{0:T(1024)S(1)} %convert_reduce_fusion), channel_id=1, replica_groups=mesh['gx'=4,'gy'=8,'gz'=8] {'gz'}, use_global_device_ids=true, to_apply=%region_5.0 | all-reduce | flops 896 | bytes 7168 | tf_op jit(solution)/shard_map/psum | solution.py:49
  344.0 0.0 reduce-scatter.11.cloned.1.call-done
  344.0 75.5 %reduce-scatter.13.cloned.1.call-done = bf16[448,896]{1,0:T(8,128)(2,1)} async-done(((bf16[3584,896]{1,0:T(8,128)(2,1)}), bf16[448,896]{1,0:T(8,128)(2,1)}) %reduce-scatter.13.cloned.1.call-update) | async-done | bytes 802832
  419.5 82.2 %reduce-scatter.15.cloned.1.call-done = bf16[448,896]{1,0:T(8,128)(2,1)} async-done(((bf16[3584,896]{1,0:T(8,128)(2,1)}), bf16[448,896]{1,0:T(8,128)(2,1)}) %reduce-scatter.15.cloned.1.call-update) | async-done | bytes 802832
Async XLA Ops:
  7.2 53.2 %all-gather.5.cloned.1.call-start = ((), (), s32[]{:S(2)}) async-start(), calls=%async_computation.4 | async-start | bytes 2064384 | tf_op jit(solution)/shard_map/all_gather | solution.py:33
  7.9 126.6 %all-gather.7.cloned.1.call-start = ((), (), s32[]{:S(2)}) async-start(), calls=%async_computation.5 | async-start | bytes 7225344 | tf_op jit(solution)/shard_map/all_gather | solution.py:37
  8.6 154.5 %copy-start.1 = (bf16[64,896]{1,0:T(8,128)(2,1)S(1)}, bf16[64,896]{1,0:T(8,128)(2,1)}, u32[]{:S(2)}) copy-start(bf16[64,896]{1,0:T(8,128)(2,1)} %param.6) | copy-start | bytes 344068
  8.7 154.5 %reduce-scatter.9.cloned.1.call-start = ((), (), s32[]{:S(2)}) async-start(), calls=%async_computation.6 | async-start | bytes 573440 | tf_op jit(solution)/shard_map/reduce_scatter | solution.py:39
  140.8 95.1 %all-gather.9.cloned.1.call-start = ((), (), s32[]{:S(2)}) async-start(), calls=%async_computation.7 | async-start | bytes 7225344 | tf_op jit(solution)/shard_map/all_gather | solution.py:58
  141.4 142.8 %all-gather.11.cloned.1.call-start = ((), (), s32[]{:S(2)}) async-start(), calls=%async_computation.9 | async-start | bytes 2064384 | tf_op jit(solution)/shard_map/all_gather | solution.py:32
  141.9 202.0 %reduce-scatter.11.cloned.1.call-start = ((), (), s32[]{:S(2)}) async-start(), calls=%async_computation.8 | async-start | bytes 2064384 | tf_op jit(solution)/shard_map/reduce_scatter | solution.py:61
  242.1 177.4 %reduce-scatter.13.cloned.1.call-start = ((), (), s32[]{:S(2)}) async-start(), calls=%async_computation.10 | async-start | bytes 7225344
  299.8 13.2 %copy-start = (bf16[256,3584]{1,0:T(8,128)(2,1)S(1)}, bf16[256,3584]{1,0:T(8,128)(2,1)}, u32[]{:S(2)}) copy-start(bf16[256,3584]{1,0:T(8,128)(2,1)} %all-gather.5.cloned.1.call-done) | copy-start | bytes 5505028
  299.8 201.9 %reduce-scatter.15.cloned.1.call-start = ((), (), s32[]{:S(2)}) async-start(), calls=%async_computation.11 | async-start | bytes 7225344
Sparse Core Ops, SparseCore 0:
  9.8 50.5 all-gather.4
  62.2 72.2 all-gather.6
  140.9 22.1 reduce-scatter.8
  164.9 70.9 all-gather.8
  237.7 46.4 all-gather.10
  287.4 49.5 reduce-scatter.10
  340.2 79.2 reduce-scatter.12
  422.6 78.9 reduce-scatter.14
where the time goes:
time: 511 us; the launch traced here: 508 us
  waiting for transfers between devices  408 us (80%)
  blocking collectives  42.6 us (8%)
  matrix products  22.9 us (4%)
  local copies, waits for them, and re-layouts  19.1 us (4%)
  between operations  14.2 us (3%)
    unnamed x10, waiting for transfers between devices  160 us
    all_gather x1, waiting for transfers between devices, shards(): lax.all_gather(w_out, 'gz', axis=0, tiled=True)  74.2 us
    all_gather x1, waiting for transfers between devices, shards(): lax.all_gather(w_in, 'gz', axis=0, tiled=True)  59.1 us
    all_gather x1, waiting for transfers between devices, shards(): lax.all_gather(out_grad, 'gy', axis=0, tiled=True)  51.7 us
    all_gather x1, waiting for transfers between devices, shards(): lax.all_gather(acts, 'gy', axis=0, tiled=True)  42 us
    reduce_scatter x1, waiting for transfers between devices, shards(): lax.psum_scatter(partial_hidden.astype(jnp.bfloat16), 'gx', scatter_dimen...  21.1 us
    unnamed x6, local copies, waits for them, and re-layouts  19.1 us
    psum x1, blocking collectives, shards(): bias_grad = lax.psum(jnp.sum(dh_rows.astype(jnp.float32), axis=0), 'gz')  16.9 us
  transfers between devices with their start and end apart: 8, of which 7 were waited for; matrix products, arithmetic and copies ran while one was open for 7% of the time, Pallas kernels for 0%

commit v1 on v0

v1 whole, which is shorter than its diff:
```python
import jax
import jax.numpy as jnp
from jax import lax
from jax.sharding import PartitionSpec as P


def gelu_parts(pre):
    coeff = 0.7978845608028654
    inner = coeff * (pre + 0.044715 * pre * pre * pre)
    tangent = jnp.tanh(inner)
    value = 0.5 * pre * (1.0 + tangent)
    slope = 0.5 * (1.0 + tangent) + 0.5 * pre * (1.0 - tangent * tangent) * coeff * (
        1.0 + 3.0 * 0.044715 * pre * pre
    )
    return (value, slope)


def left_product(left, right):
    return lax.dot_general(
        left, right, (((0,), (0,)), ((), ())), preferred_element_type=jnp.float32
    )


def right_product(left, right):
    return lax.dot_general(
        left, right, (((1,), (1,)), ((), ())), preferred_element_type=jnp.float32
    )


def slice_rows(rows):
    mine = lax.all_to_all(rows, "gz", split_axis=1, concat_axis=0, tiled=True)
    every = lax.all_gather(mine.reshape(8, 1, 32, -1), "gy", axis=1, tiled=True)
    return every.reshape(2048, -1)


def shards(acts, preact, out_grad, w_in, w_out):
    value, slope = gelu_parts(preact.astype(jnp.float32))
    act_rows = lax.all_gather(value.astype(jnp.bfloat16), ("gz", "gx"), axis=0, tiled=True)
    grad_rows = slice_rows(out_grad)
    partial_hidden = jnp.dot(grad_rows, w_out, preferred_element_type=jnp.float32)
    hidden_grad = lax.psum_scatter(
        partial_hidden.astype(jnp.bfloat16), ("gz", "gx"), scatter_dimension=0, tiled=True
    ).astype(jnp.float32)
    acts_rows = slice_rows(acts)
    dh_local = (hidden_grad * slope).astype(jnp.bfloat16)
    dh_rows = lax.all_gather(dh_local, ("gz", "gx"), axis=0, tiled=True)
    partial_input = right_product(dh_rows, w_in).astype(jnp.bfloat16)
    summed = lax.psum_scatter(
        partial_input.reshape(8, 8, 32, -1), "gy", scatter_dimension=1, tiled=True
    )
    input_grad = lax.all_to_all(
        summed.reshape(256, -1), "gz", split_axis=0, concat_axis=1, tiled=True
    )
    bias_grad = jnp.sum(dh_rows.astype(jnp.float32), axis=0)
    out_weight_grad = left_product(grad_rows, act_rows).astype(jnp.bfloat16)
    in_weight_grad = left_product(acts_rows, dh_rows).astype(jnp.bfloat16)
    return (input_grad, in_weight_grad, out_weight_grad, bias_grad)


def solution(mesh):
    return jax.shard_map(
        shards,
        mesh=mesh,
        in_specs=(
            P(("gz", "gy"), "gx"),
            P(("gz", "gx"), "gy"),
            P(("gz", "gy"), "gx"),
            P(("gx", "gz"), "gy"),
            P(("gx", "gz"), "gy"),
        ),
        out_specs=(P(("gz", "gy"), "gx"), P(("gx", "gz"), "gy"), P(("gx", "gz"), "gy"), P("gy")),
        check_vma=False,
    )
```

time: 511 us -> 504 us (0.986)
  waiting for transfers between devices: 408 us -> 401 us
  starting transfers between devices: 0.31 us -> 7.26 us
  blocking collectives: 42.6 us -> 37.2 us
    reduce_scatter x2 -> x1, waiting for transfers between devices: 21.1 us -> 97.4 us  [shards(): lax.psum_scatter(partial_hidden.astype(jnp.bfloat16), ('gz', 'gx'), scatt...]
    unnamed x10 -> x7, waiting for transfers between devices: 160 us -> 105 us
    all_to_all x0 -> x2, blocking collectives: none -> 37.2 us  [slice_rows(): mine = lax.all_to_all(rows, 'gz', split_axis=1, concat_axis=0, tiled=True)]
    all_gather x4, waiting for transfers between devices: 227 us -> 192 us  [the longest x2 97.3 us: slice_rows(): every = lax.all_gather(mine.reshape(8, 1, 32, -1), 'gy', axis=1, tiled=True)]
    all_gather x2 -> x0, blocking collectives: 25.7 us -> none  [the longest x1 13.1 us: shards(): lax.all_gather(act_local, 'gx', axis=0, tiled=True)]
    psum x1 -> x0, blocking collectives: 16.9 us -> none  [shards(): bias_grad = lax.psum(jnp.sum(dh_rows.astype(jnp.float32), axis=0), 'gz')]
    unnamed x6 -> x19, local copies, waits for them, and re-layouts: 19.1 us -> 4.35 us
    all_gather x0 -> x2, local copies, waits for them, and re-layouts: none -> 7.87 us  [slice_rows(): every = lax.all_gather(mine.reshape(8, 1, 32, -1), 'gy', axis=1, tiled=True)]
  transfers between devices with their start and end apart: 8 -> 7, of which waited for: 7 -> 7; matrix products, arithmetic and copies ran while one was open for 7% -> 5% of each run, Pallas kernels for 0% -> 0%
where the time goes in v1:
time: 504 us; the launch traced here: 503 us
  waiting for transfers between devices  401 us (80%)
  blocking collectives  37.2 us (7%)
  local copies, waits for them, and re-layouts  21.6 us (4%)
  matrix products  19 us (4%)
  between operations  14.2 us (3%)
  starting transfers between devices  7.26 us (1%)
    unnamed x7, waiting for transfers between devices  105 us
    reduce_scatter x1, waiting for transfers between devices, shards(): lax.psum_scatter(partial_hidden.astype(jnp.bfloat16), ('gz', 'gx'), scatt...  97.4 us
    all_gather x2, waiting for transfers between devices, slice_rows(): every = lax.all_gather(mine.reshape(8, 1, 32, -1), 'gy', axis=1, tiled=True)  97.3 us
    all_gather x1, waiting for transfers between devices, shards(): lax.all_gather(value.astype(jnp.bfloat16), ('gz', 'gx'), axis=0, tiled=True)  56.2 us
    all_gather x1, waiting for transfers between devices, shards(): dh_rows = lax.all_gather(dh_local, ('gz', 'gx'), axis=0, tiled=True)  38.5 us
    all_to_all x2, blocking collectives, slice_rows(): mine = lax.all_to_all(rows, 'gz', split_axis=1, concat_axis=0, tiled=True)  37.2 us
    dot_general x2, matrix products, left_product(): lax.dot_general(left, right, (((0,), (0,)), ((), ())), preferred_element_...  10.7 us
  transfers between devices with their start and end apart: 7, of which 7 were waited for; matrix products, arithmetic and copies ran while one was open for 5% of the time, Pallas kernels for 0%

profile of v1, /device:TPU:32, one launch (start us, length us, event | category | flops | bytes accessed | tf_op | source)
XLA Modules:
  0.0 502.7 jit_solution(18000440620681732887)
XLA Ops:
  7.2 0.0 copy-start
  7.2 0.0 all-gather.11.cloned.1.call-start
  7.2 1.3 all_to_all.38
  8.6 0.1 copy.23
  8.7 19.8 %all_to_all.51 = bf16[32,8,448]{2,0,1:T(8,128)(2,1)S(1)} all-to-all(bf16[32,8,448]{2,0,1:T(8,128)(2,1)S(1)} %copy.23), channel_id=1, replica_groups=mesh['gx'=4,'gy'=8,'gz'=8] {'gz'}, dimensions={1} | all-to-all | bytes 458752 | tf_op jit(solution)/shard_map/all_to_all | solution.py:31
  28.4 0.9 copy.24
  29.3 0.0 all-gather.11.cloned.1.call-update
  29.3 0.0 reduce-scatter.3.cloned.1.call-start
  29.3 50.3 %all-gather.11.cloned.1.call-done = bf16[8,256,448]{2,0,1:T(8,128)(2,1)} async-done(((bf16[8,32,448]{2,0,1:T(8,128)(2,1)}), bf16[8,256,448]{2,0,1:T(8,128)(2,1)}) %all-gather.11.cloned.1.call-update) | async-done | bytes 1835024 | tf_op jit(solution)/shard_map/all_gather | solution.py:32
  79.6 3.9 copy.25
  83.6 0.6 copy.33
  84.2 0.0 copy-start.2
  84.2 1.2 copy-done.2
  85.4 0.0 copy-done
  85.4 4.2 convolution_convert_fusion
  89.6 0.0 copy-start.5
  89.6 0.0 copy-start.4
  89.6 0.0 reduce-scatter.3.cloned.1.call-update
  89.6 0.0 copy-start.6
  89.6 0.0 all-gather.7.cloned.1.call-start
  89.7 97.4 %reduce-scatter.3.cloned.1.call-done = bf16[64,896]{1,0:T(8,128)(2,1)} async-done(((bf16[2048,896]{1,0:T(8,128)(2,1)}), bf16[64,896]{1,0:T(8,128)(2,1)}) %reduce-scatter.3.cloned.1.call-update) | async-done | bytes 114704 | tf_op jit(solution)/shard_map/reduce_scatter | solution.py:41
  187.1 0.0 copy-done.5
  187.1 1.8 fusion.9
  188.8 0.0 all-gather.7.cloned.1.call-update
  188.8 0.0 all-gather.13.cloned.1.call-start
  188.9 0.0 copy-done.4
  188.9 0.3 all_to_all.45
  189.2 0.1 copy.28
  189.3 17.4 %all_to_all.52 = bf16[32,8,448]{2,0,1:T(8,128)(2,1)S(1)} all-to-all(bf16[32,8,448]{2,0,1:T(8,128)(2,1)S(1)} %copy.28), channel_id=1, replica_groups=mesh['gx'=4,'gy'=8,'gz'=8] {'gz'}, dimensions={1} | all-to-all | bytes 458752 | tf_op jit(solution)/shard_map/all_to_all | solution.py:31
  206.7 0.9 copy.29
  207.6 0.0 all-gather.13.cloned.1.call-update
  207.6 0.0 all-gather.9.cloned.1.call-start
  207.6 0.5 all-gather.9.cloned.1.call-update
  208.2 0.0 all-reduce.3.cloned.1.call-start
  208.2 38.5 %all-gather.7.cloned.1.call-done = bf16[2048,896]{1,0:T(8,128)(2,1)} async-done(((bf16[64,896]{1,0:T(8,128)(2,1)}), bf16[2048,896]{1,0:T(8,128)(2,1)}) %all-gather.7.cloned.1.call-update) | async-done | bytes 3670032 | tf_op jit(solution)/shard_map/all_gather | solution.py:46
  246.7 0.0 copy-done.6
  246.7 4.1 convolution_convert_fusion.1
  250.9 0.0 copy-start.7
  250.9 2.4 copy.26
  253.3 0.0 all-reduce.3.cloned.1.call-update
  253.3 0.0 copy-done.7
  253.3 0.6 dynamic-slice
  253.9 47.0 %all-gather.13.cloned.1.call-done = bf16[8,256,448]{2,0,1:T(8,128)(2,1)} async-done(((bf16[8,32,448]{2,0,1:T(8,128)(2,1)}), bf16[8,256,448]{2,0,1:T(8,128)(2,1)}) %all-gather.13.cloned.1.call-update) | async-done | bytes 1835024 | tf_op jit(solution)/shard_map/all_gather | solution.py:32
  300.9 3.9 copy.30
  304.9 1.9 copy.34
  306.8 0.0 copy-start.3
  306.8 56.2 %all-gather.9.cloned.1.call-done = bf16[2048,896]{1,0:T(8,128)(2,1)} async-done(((bf16[64,896]{1,0:T(8,128)(2,1)}), bf16[2048,896]{1,0:T(8,128)(2,1)}) %all-gather.9.cloned.1.call-update) | async-done | bytes 3670032 | tf_op jit(solution)/shard_map/all_gather | solution.py:38
  363.0 5.5 %fusion.1 = bf16[448,896]{1,0:T(8,128)(2,1)} fusion(bf16[2048,448]{0,1:T(8,128)(2,1)} %bitcast.35, bf16[2048,896]{1,0:T(8,128)(2,1)} %all-gather.9.cloned.1.call-done), kind=kOutput, calls=%fused_computation.6 | convolution fusion | flops 1644568576 | bytes 6307840 | tf_op jit(solution)/shard_map/dot_general | solution.py:19
  368.5 104.1 %all-reduce.3.cloned.1.call-done = bf16[8,8,32,448]{3,2,1,0:T(8,128)(2,1)} async-done(((bf16[8,8,32,448]{3,2,1,0:T(8,128)(2,1)}), bf16[8,8,32,448]{3,2,1,0:T(8,128)(2,1)}) %all-reduce.3.cloned.1.call-update) | async-done | bytes 1835024
  472.6 2.3 dynamic-slice_bitcast_fusion
  475.0 7.0 %all-to-all-start.1 = ((bf16[8,32,448]{2,1,0:T(8,128)(2,1)}), bf16[8,32,448]{2,1,0:T(8,128)(2,1)S(1)}, u32[]{:S(2)}, u32[]{:S(2)}) async-start(bf16[8,32,448]{2,1,0:T(8,128)(2,1)} %dynamic-slice_bitcast_fusion), calls=%async_computation.2 | async-start | bytes 524288 | tf_op jit(solution)/shard_map/all_to_all | solution.py:51
  482.0 0.0 copy-done.3
  482.0 0.0 copy-start.1
  482.0 5.1 %fusion = bf16[448,896]{1,0:T(8,128)(2,1)} fusion(bf16[2048,448]{0,1:T(8,128)(2,1)S(1)} %bitcast.36, bf16[2048,896]{1,0:T(8,128)(2,1)} %all-gather.7.cloned.1.call-done), kind=kOutput, calls=%fused_computation.5 | convolution fusion | flops 1644568576 | bytes 6307840 | tf_op jit(solution)/shard_map/dot_general | solution.py:19
  487.1 0.0 copy-done.1
  487.1 1.2 convert_reduce_fusion
  488.3 6.4 %all-to-all-done.1 = bf16[8,32,448]{2,1,0:T(8,128)(2,1)S(1)} async-done(((bf16[8,32,448]{2,1,0:T(8,128)(2,1)}), bf16[8,32,448]{2,1,0:T(8,128)(2,1)S(1)}, u32[]{:S(2)}, u32[]{:S(2)}) %all-to-all-start.1) | async-done | bytes 229408 | tf_op jit(solution)/shard_map/all_to_all | solution.py:51
  494.7 0.1 copy.27
  494.9 1.0 all_to_all.44
Async XLA Ops:
  7.2 78.2 %copy-start = (bf16[448,896]{1,0:T(8,128)(2,1)S(1)}, bf16[448,896]{1,0:T(8,128)(2,1)}, u32[]{:S(2)}) copy-start(bf16[448,896]{1,0:T(8,128)(2,1)} %param.9) | copy-start | bytes 2408452
  7.2 72.5 %all-gather.11.cloned.1.call-start = ((), (), s32[]{:S(2)}) async-start(), calls=%async_computation.7 | async-start | bytes 2359296 | tf_op jit(solution)/shard_map/all_gather | solution.py:32
  29.3 157.8 %reduce-scatter.3.cloned.1.call-start = ((), (), s32[]{:S(2)}) async-start(), calls=%async_computation.4 | async-start | bytes 3784704 | tf_op jit(solution)/shard_map/reduce_scatter | solution.py:41
  84.2 1.2 copy-start.2
  89.6 97.5 %copy-start.5 = (bf16[64,896]{1,0:T(8,128)(2,1)S(1)}, bf16[64,896]{1,0:T(8,128)(2,1)}, u32[]{:S(2)}) copy-start(bf16[64,896]{1,0:T(8,128)(2,1)} %param.6) | copy-start | bytes 344068
  89.6 99.3 %copy-start.4 = (bf16[32,3584]{1,0:T(8,128)(2,1)S(1)}, bf16[32,3584]{1,0:T(8,128)(2,1)}, u32[]{:S(2)}) copy-start(bf16[32,3584]{1,0:T(8,128)(2,1)} %param.5) | copy-start | bytes 688132
  89.6 157.1 %copy-start.6 = (bf16[448,896]{1,0:T(8,128)(2,1)S(1)}, bf16[448,896]{1,0:T(8,128)(2,1)}, u32[]{:S(2)}) copy-start(bf16[448,896]{1,0:T(8,128)(2,1)} %param.8) | copy-start | bytes 2408452
  89.6 157.1 %all-gather.7.cloned.1.call-start = ((), (), s32[]{:S(2)}) async-start(), calls=%async_computation.5 | async-start | bytes 3784704 | tf_op jit(solution)/shard_map/all_gather | solution.py:46
  188.8 112.1 %all-gather.13.cloned.1.call-start = ((), (), s32[]{:S(2)}) async-start(), calls=%async_computation.8 | async-start | bytes 2359296 | tf_op jit(solution)/shard_map/all_gather | solution.py:32
  207.6 155.4 %all-gather.9.cloned.1.call-start = ((), (), s32[]{:S(2)}) async-start(), calls=%async_computation.6 | async-start | bytes 3784704 | tf_op jit(solution)/shard_map/all_gather | solution.py:38
  208.2 264.4 %all-reduce.3.cloned.1.call-start = ((), (), s32[]{:S(2)}) async-start(), calls=%async_computation.9 | async-start | bytes 4194304
  250.9 2.5 copy-start.7
  306.8 175.2 %copy-start.3 = (bf16[56,8,8,256]{3,1,2,0:T(8,128)(2,1)S(1)}, bf16[56,8,8,256]{3,1,2,0:T(8,128)(2,1)}, u32[]{:S(2)}) copy-start(bf16[56,8,8,256]{3,1,2,0:T(8,128)(2,1)} %copy.34) | copy-start | bytes 5505028
  475.0 19.8 %all-to-all-start.1 = ((bf16[8,32,448]{2,1,0:T(8,128)(2,1)}), bf16[8,32,448]{2,1,0:T(8,128)(2,1)S(1)}, u32[]{:S(2)}, u32[]{:S(2)}) async-start(bf16[8,32,448]{2,1,0:T(8,128)(2,1)} %dynamic-slice_bitcast_fusion), calls=%async_computation.2 | async-start | bytes 524288 | tf_op jit(solution)/shard_map/all_to_all | solution.py:51
  482.0 5.1 %copy-start.1 = (bf16[2048,896]{1,0:T(8,128)(2,1)S(1)}, bf16[2048,896]{1,0:T(8,128)(2,1)}, u32[]{:S(2)}) copy-start(bf16[2048,896]{1,0:T(8,128)(2,1)} %all-gather.7.cloned.1.call-done) | copy-start | bytes 11010052
Sparse Core Ops, SparseCore 0:
  29.4 50.1 all-gather.10
  89.7 97.2 reduce-scatter.2
  190.5 56.1 all-gather.6
  249.1 51.8 all-gather.12
  304.2 58.7 all-gather.8
  365.7 106.8 all-reduce.2

commit v2 on v1

v2 whole, which is shorter than its diff:
```python
import jax
import jax.numpy as jnp
from jax import lax
from jax.experimental import pallas as pl
from jax.experimental.pallas import tpu as pltpu
from jax.sharding import PartitionSpec as P

MESH = pl.DeviceIdType.MESH
BF = jnp.bfloat16
F32 = jnp.float32
W = 896
N_SEMS = 160


def gelu_parts(pre):
    coeff = 0.7978845608028654
    inner = coeff * (pre + 0.044715 * pre * pre * pre)
    tangent = jnp.tanh(inner)
    value = 0.5 * pre * (1.0 + tangent)
    slope = 0.5 * (1.0 + tangent) + 0.5 * pre * (1.0 - tangent * tangent) * coeff * (
        1.0 + 3.0 * 0.044715 * pre * pre
    )
    return (value, slope)


def dot(left, right, dims):
    return lax.dot_general(left, right, (dims, ((), ())), preferred_element_type=F32)


class Ring:
    def __init__(self, me, device):
        self.me = me
        self.p, self.m, self.o = (lax.rem(me + k, 4) for k in (1, 3, 2))
        self.plus, self.minus = device(self.p), device(self.m)


def kernel(
    acts, pre, grad, w_in, w_out,
    o_ig, o_iw, o_ow, o_bias,
    G, A, AC, D, WO, WI,
    HP, H1, H2, HX, HS, HB, ZR, SL,
    QP, Q1, Q2, QX, QS, ZS, ZL, IS, IR,
    ACC, OWN, WS, WR, BS, BR,
    send_sem, recv_sem, local_sem,
):
    gx, gy, gz = (lax.axis_index(name) for name in ("gx", "gy", "gz"))
    y, zl = gy // 2, lax.rem(gy, 2)
    zh, core = gz // 2, lax.rem(gz, 2)
    x = gx
    other = 1 - zl

    def dev(x_=x, y_=y, zl_=zl, zh_=zh, c_=core):
        return (x_, y_ * 2 + zl_, zh_ * 2 + c_)

    up, down, opp = (lax.rem(zh + k, 4) for k in (1, 3, 2))
    near = jnp.where(zl == 0, down, up)
    far = jnp.where(zl == 0, up, down)
    order = (zh, near, far, opp)
    twin = dev(c_=1 - core)
    pair = dev(zl_=other)
    rx = Ring(x, lambda k: dev(x_=k))
    ry = Ring(y, lambda k: dev(y_=k))

    peers = [rx.plus, rx.minus, ry.plus, ry.minus, twin, pair]
    peers += [dev(zh_=k) for k in (up, down, opp)]
    peers += [dev(zl_=other, zh_=near), dev(zl_=other, zh_=opp)]
    barrier = pltpu.get_barrier_semaphore()
    for peer in peers:
        pl.semaphore_signal(barrier, inc=1, device_id=peer, device_id_type=MESH)
    pl.semaphore_wait(barrier, len(peers))

    count = [0]
    sends = []

    def sem():
        count[0] += 1
        return count[0] - 1

    def send(k, src, dst, to):
        copy = pltpu.make_async_remote_copy(
            src_ref=src, dst_ref=dst, send_sem=send_sem.at[k], recv_sem=recv_sem.at[k],
            device_id=to, device_id_type=MESH,
        )
        copy.start()
        sends.append(copy)

    def arrived(k, dst):
        pltpu.make_async_remote_copy(
            src_ref=dst, dst_ref=dst, send_sem=send_sem.at[k], recv_sem=recv_sem.at[k],
            device_id=twin, device_id_type=MESH,
        ).wait_recv()

    n_local = [0]

    def local(src, dst):
        copy = pltpu.make_async_copy(src, dst, local_sem.at[n_local[0]])
        n_local[0] += 1
        copy.start()
        return copy

    def half(k):
        return pl.ds(pl.multiple_of(k * 32, 32), 32)

    LO, HI = pl.ds(0, 32), pl.ds(32, 32)

    class Rows:
        def __init__(self, src, buf):
            self.src, self.buf = src, buf
            self.k = [sem() for _ in range(6)]

        def columns(self, k):
            return self.src.at[:, pl.ds(pl.multiple_of(k * W, W), W)]

        def scatter(self):
            k, here = self.k, self.buf.at[zh, y, half(zl)]
            self.own = local(self.columns(zh), here)
            send(k[0], self.columns(zh), here, pair)
            send(k[1], self.columns(far), here, dev(zh_=far))
            send(k[2], self.columns(near), here, dev(zl_=other, zh_=near))
            send(k[3], self.columns(opp), here, dev(zl_=other, zh_=opp))

        def ready(self, t):
            k, buf = self.k, self.buf
            if t == 0:
                self.own.wait()
                arrived(k[0], buf.at[zh, y, half(other)])
            elif t == 1:
                arrived(k[1], buf.at[near, y, half(zl)])
                arrived(k[2], buf.at[near, y, half(other)])
                send(k[4], buf.at[near, y], buf.at[near, y], pair)
            elif t == 2:
                arrived(k[4], buf.at[far, y])
            else:
                piece = buf.at[opp, y, half(other)]
                arrived(k[3], piece)
                send(k[5], piece, piece, pair)
                arrived(k[5], buf.at[opp, y, half(zl)])

    class Gather:
        def __init__(self, buf, ring, s):
            self.buf, self.ring, self.s = buf, ring, s
            self.k = [sem() for _ in range(4)]

        def at(self, block, rows=pl.ds(0, 64)):
            return self.buf.at[self.s, block, rows]

        def start(self):
            r, mine = self.ring, self.at(self.ring.me)
            send(self.k[0], mine, mine, r.plus)
            send(self.k[1], mine, mine, r.minus)

        def forward(self):
            r = self.ring
            arrived(self.k[0], self.at(r.m))
            send(self.k[2], self.at(r.m, LO), self.at(r.m, LO), r.plus)
            arrived(self.k[1], self.at(r.p))
            send(self.k[3], self.at(r.p, HI), self.at(r.p, HI), r.minus)

        def done(self):
            r = self.ring
            arrived(self.k[2], self.at(r.o, LO))
            arrived(self.k[3], self.at(r.o, HI))

    class Scatter:
        def __init__(self, part, first, second, mixed, ring, t):
            self.part, self.first, self.second, self.mixed = (
                part.at[t], first.at[t], second.at[t], mixed.at[t]
            )
            self.ring = ring
            self.k = [sem() for _ in range(6)]

        def start(self):
            r, k = self.ring, self.k
            send(k[0], self.part.at[r.o, LO], self.first.at[0], r.plus)
            send(k[1], self.part.at[r.o, HI], self.first.at[1], r.minus)
            send(k[2], self.part.at[r.p, HI], self.second.at[0, HI], r.plus)
            send(k[3], self.part.at[r.m, LO], self.second.at[1, LO], r.minus)

        def middle(self):
            r, k = self.ring, self.k
            for way, rows, block, to in ((0, LO, r.p, r.plus), (1, HI, r.m, r.minus)):
                arrived(k[way], self.first.at[way])
                total = self.part[block, rows].astype(F32) + self.first[way].astype(F32)
                self.mixed[way] = total.astype(BF)
                send(k[4 + way], self.mixed.at[way], self.second.at[way, rows], to)

        def end(self):
            k = self.k
            arrived(k[2], self.second.at[0, HI])
            arrived(k[3], self.second.at[1, LO])
            arrived(k[4], self.second.at[0, LO])
            arrived(k[5], self.second.at[1, HI])
            return (
                self.part[self.ring.me].astype(F32)
                + self.second[0].astype(F32)
                + self.second[1].astype(F32)
            )

    class Depth:
        def __init__(self, buf):
            self.buf = buf
            self.k = [sem() for _ in range(3)]

        def start(self):
            mine = self.buf.at[zh, x]
            for k, to in zip(self.k, (near, far, opp)):
                send(k, mine, mine, dev(zh_=to))

        def ready(self, t):
            k = self.k[(None, 1, 0, 2)[t]]
            arrived(k, self.buf.at[order[t], x])

    rows_g, rows_a = Rows(grad, G), Rows(acts, A)
    g_y = [Gather(G, ry, s) for s in order]
    a_y = Gather(A, ry, pl.ds(0, 4))
    c_z, c_x = Depth(AC), Gather(AC, rx, pl.ds(0, 4))
    h_x = [Scatter(HP, H1, H2, HX, rx, t) for t in range(4)]
    h_k = [sem() for _ in range(3)]
    d_z, d_x = Depth(D), [Gather(D, rx, s) for s in order]
    q_y = [Scatter(QP, Q1, Q2, QX, ry, t) for t in range(4)]
    q_k = [sem() for _ in range(4)]
    i_k = [sem() for _ in range(3)]
    w_k = [sem() for _ in range(2)]
    g_k = [sem() for _ in range(2)]
    b_k = sem()

    mine = pl.ds(pl.multiple_of(core * 448, 448), 448)
    theirs = pl.ds(pl.multiple_of((1 - core) * 448, 448), 448)

    rows_g.scatter()
    own_w = []
    for k, src, buf in ((w_k[0], w_out, WO), (w_k[1], w_in, WI)):
        send(k, src, buf.at[mine], twin)
        own_w.append(local(src, buf.at[mine]))

    value, slope = gelu_parts(pre[...].astype(F32))
    AC[zh, x] = value.astype(BF)
    SL[...] = slope

    def hidden(t):
        g_y[t].done()
        if t == 0:
            own_w[0].wait()
            arrived(w_k[0], WO.at[theirs])
        part = dot(G[order[t]].reshape(256, W), WO[...], ((1,), (0,)))
        HP[t] = part.astype(BF).reshape(4, 64, W)
        h_x[t].start()

    def hidden_end(t):
        total = h_x[t].end()
        if t == 0:
            HS[3] = total
        else:
            HB[t - 1] = total.astype(BF)
            send(h_k[t - 1], HB.at[t - 1], ZR.at[t - 1], dev(zh_=order[t]))

    rows_g.ready(0)
    g_y[0].start()
    rows_g.ready(1)
    g_y[1].start()
    g_y[0].forward()
    rows_g.ready(2)
    g_y[2].start()
    g_y[1].forward()
    rows_g.ready(3)
    g_y[3].start()
    c_z.start()
    rows_a.scatter()
    hidden(0)
    g_y[2].forward()
    hidden(1)
    h_x[0].middle()
    g_y[3].forward()
    hidden(2)
    h_x[1].middle()
    hidden_end(0)
    for t in range(4):
        rows_a.ready(t)
    a_y.start()
    hidden(3)
    h_x[2].middle()
    hidden_end(1)
    h_x[3].middle()
    for t in range(1, 4):
        c_z.ready(t)
    c_x.start()
    hidden_end(2)
    hidden_end(3)
    a_y.forward()

    total = HS[3]
    for t in range(3):
        arrived(h_k[t], ZR.at[t])
        total = total + ZR[t].astype(F32)
    D[zh, x] = (total * SL[...]).astype(BF)
    d_x[0].start()
    d_z.start()

    def weight_grad(rows, cols, t, first):
        right = cols[order[t]].reshape(256, W)

        def step(i, carry):
            at = pl.ds(pl.multiple_of(i * 128, 128), 128)
            left = rows[order[t], :, :, at].reshape(256, 128)
            term = dot(left, right, ((0,), (0,)))
            if first:
                ACC[at] = term
            else:
                ACC[at] += term
            return carry

        lax.fori_loop(0, 7, step, 0)

    def share(i):
        WS[i] = ACC[theirs].astype(BF)
        send(g_k[i], WS.at[i], WR.at[i], twin)
        OWN[i] = ACC[mine]

    def inputs(t):
        d_x[t].done()
        if t == 0:
            own_w[1].wait()
            arrived(w_k[1], WI.at[theirs])
        part = dot(D[order[t]].reshape(256, W), WI[...], ((1,), (1,)))
        QP[t] = part.astype(BF).reshape(4, 64, W)
        q_y[t].start()

    def inputs_end(t):
        QS[t] = q_y[t].end()
        ZS[t] = QS[t, half(other)].astype(BF)
        there = (0, 2, 1, 3)[t]
        send(q_k[there], ZS.at[t], ZL.at[there], pair)

    def inputs_out(t):
        arrived(q_k[t], ZL.at[t])
        total = (QS[t, half(zl)] + ZL[t].astype(F32)).astype(BF)
        if t == 0:
            IR[zh] = total
        else:
            IS[t] = total
            send(i_k[t - 1], IS.at[t], IR.at[zh], dev(zh_=order[t]))

    d_z.ready(1)
    d_x[1].start()
    d_x[0].forward()
    d_z.ready(2)
    d_x[2].start()
    d_x[1].forward()
    d_z.ready(3)
    d_x[3].start()
    inputs(0)
    d_x[2].forward()
    inputs(1)
    q_y[0].middle()
    d_x[3].forward()
    c_x.forward()
    a_y.done()
    weight_grad(A, D, 0, True)
    inputs(2)
    q_y[1].middle()
    inputs_end(0)
    weight_grad(A, D, 1, False)
    inputs(3)
    q_y[2].middle()
    inputs_end(1)
    inputs_out(0)
    weight_grad(A, D, 2, False)
    q_y[3].middle()
    inputs_end(2)
    inputs_out(1)
    weight_grad(A, D, 3, False)
    share(0)
    inputs_end(3)
    inputs_out(2)
    sums = jnp.sum(D[...].astype(F32).reshape(128, 8, W), axis=0)
    BS[...] = sums
    send(b_k, BS, BR, twin)
    inputs_out(3)
    c_x.done()
    for t in range(4):
        weight_grad(G, AC, t, t == 0)
    share(1)

    for t in range(1, 4):
        arrived(i_k[(None, 1, 0, 2)[t] ], IR.at[order[t]])
    for k in range(4):
        o_ig[:, k * W : (k + 1) * W] = IR[k]
    arrived(b_k, BR)
    o_bias[...] = jnp.sum(BS[...] + BR[...], axis=0, keepdims=True)
    for i, out in ((0, o_iw), (1, o_ow)):
        arrived(g_k[i], WR.at[i])
        out[...] = (OWN[i] + WR[i].astype(F32)).astype(BF)
    for copy in sends:
        copy.wait_send()


def shards(acts, preact, out_grad, w_in, w_out):
    vmem = pl.BlockSpec(memory_space=pltpu.VMEM)
    bf = lambda *shape: pltpu.VMEM(shape, BF)
    f32 = lambda *shape: pltpu.VMEM(shape, F32)
    scratch = dict(
        G=bf(4, 4, 64, W), A=bf(4, 4, 64, W), AC=bf(4, 4, 64, W), D=bf(4, 4, 64, W),
        WO=bf(W, W), WI=bf(W, W),
        HP=bf(4, 4, 64, W), H1=bf(4, 2, 32, W), H2=bf(4, 2, 64, W), HX=bf(4, 2, 32, W),
        HS=f32(4, 64, W), HB=bf(3, 64, W), ZR=bf(3, 64, W), SL=f32(64, W),
        QP=bf(4, 4, 64, W), Q1=bf(4, 2, 32, W), Q2=bf(4, 2, 64, W), QX=bf(4, 2, 32, W),
        QS=f32(4, 64, W), ZS=bf(4, 32, W), ZL=bf(4, 32, W), IS=bf(4, 32, W), IR=bf(4, 32, W),
        ACC=f32(W, W), OWN=f32(2, 448, W), WS=bf(2, 448, W), WR=bf(2, 448, W),
        BS=f32(8, W), BR=f32(8, W),
        send_sem=pltpu.SemaphoreType.DMA((N_SEMS,)),
        recv_sem=pltpu.SemaphoreType.DMA((N_SEMS,)),
        local_sem=pltpu.SemaphoreType.DMA((8,)),
    )
    input_grad, in_weight_grad, out_weight_grad, bias_grad = pl.pallas_call(
        kernel,
        out_shape=(
            jax.ShapeDtypeStruct((32, 4 * W), BF),
            jax.ShapeDtypeStruct((448, W), BF),
            jax.ShapeDtypeStruct((448, W), BF),
            jax.ShapeDtypeStruct((1, W), F32),
        ),
        in_specs=[vmem] * 5,
        out_specs=[vmem] * 4,
        scratch_shapes=list(scratch.values()),
        compiler_params=pltpu.CompilerParams(
            collective_id=0, has_side_effects=True, vmem_limit_bytes=60 * 2**20
        ),
    )(acts, preact, out_grad, w_in, w_out)
    return (input_grad, in_weight_grad, out_weight_grad, bias_grad.reshape(W))


def solution(mesh):
    return jax.shard_map(
        shards,
        mesh=mesh,
        in_specs=(
            P(("gz", "gy"), "gx"),
            P(("gz", "gx"), "gy"),
            P(("gz", "gy"), "gx"),
            P(("gx", "gz"), "gy"),
            P(("gx", "gz"), "gy"),
        ),
        out_specs=(P(("gz", "gy"), "gx"), P(("gx", "gz"), "gy"), P(("gx", "gz"), "gy"), P("gy")),
        check_vma=False,
    )
```

time: 504 us -> 125 us (0.25)
  the two profiles are of different devices: /device:TPU:32 before, /device:TPU:1 now
where the time goes in v2:
time: 125 us
  Pallas kernels  118 us (94%)
  local copies, waits for them, and re-layouts  5.35 us (4%)
    pallas_call x1, Pallas kernels, shards(): pl.pallas_call(kernel, out_shape=(jax.ShapeDtypeStruct((32, 4 * W), BF),...  118 us
    unnamed x7, local copies, waits for them, and re-layouts  5.35 us

profile of v2, /device:TPU:1, one launch (start us, length us, event | category | flops | bytes accessed | tf_op | source)
XLA Modules:
  0.0 125.0 jit_solution(12957329642523301820)
XLA Ops:
  0.6 118.4 %shard_map.84 = (bf16[32,3584]{1,0:T(8,128)(2,1)}, bf16[448,896]{1,0:T(8,128)(2,1)}, bf16[448,896]{1,0:T(8,128)(2,1)}, f32[1,896]{1,0:T(1,128)}) custom-call(bf16[32,3584]{1,0:T(8,128)(2,1)} %acts.1, bf16[64,896]{1,0:T(8,128)(2,1)} %pre.1, bf16[32,3584]{1,0:T(8,128)(2,1)} %grad.1, bf16[448,896]{1,0:T(8,128)(2,1)} %w_in.1, bf16[448,896]{1,0:T(8,128)(2,1)} %w_out.1), custom_call_target="tpu_custom_call" | custom-call | tf_op jit(solution)/shard_map/pallas_call | solution.py:414
  119.1 0.0 copy-start.1
  119.1 0.7 copy-done.1
  119.7 0.6 reduce
  120.3 1.6 %copy.12 = bf16[32,3584]{1,0:T(8,128)(2,1)} copy(bf16[32,3584]{1,0:T(8,128)(2,1)} %get-tuple-element.16) | data formatting | bytes 458752
  122.0 0.0 copy-start
  122.0 2.2 %copy.13 = bf16[448,896]{1,0:T(8,128)(2,1)} copy(bf16[448,896]{1,0:T(8,128)(2,1)} %get-tuple-element.17) | data formatting | bytes 1605632
  124.1 0.0 copy-done
  124.1 0.9 copy.14
Async XLA Ops:
  119.1 0.7 copy-start.1
  122.0 2.2 %copy-start = (bf16[448,896]{1,0:T(8,128)(2,1)S(1)}, bf16[448,896]{1,0:T(8,128)(2,1)}, u32[]{:S(2)}) copy-start(bf16[448,896]{1,0:T(8,128)(2,1)} %get-tuple-element.18) | copy-start | bytes 2408452

commit v3 on v2

v3 whole, which is shorter than its diff:
```python
import jax
import jax.numpy as jnp
from jax import lax
from jax.experimental import pallas as pl
from jax.experimental.pallas import tpu as pltpu
from jax.sharding import PartitionSpec as P

MESH = pl.DeviceIdType.MESH
BF = jnp.bfloat16
F32 = jnp.float32
W = 896
N_SEMS = 160


def gelu_parts(pre):
    coeff = 0.7978845608028654
    inner = coeff * (pre + 0.044715 * pre * pre * pre)
    tangent = jnp.tanh(inner)
    value = 0.5 * pre * (1.0 + tangent)
    slope = 0.5 * (1.0 + tangent) + 0.5 * pre * (1.0 - tangent * tangent) * coeff * (
        1.0 + 3.0 * 0.044715 * pre * pre
    )
    return (value, slope)


def dot(left, right, dims):
    return lax.dot_general(left, right, (dims, ((), ())), preferred_element_type=F32)


class Ring:
    def __init__(self, me, device):
        self.me = me
        self.p, self.m, self.o = (lax.rem(me + k, 4) for k in (1, 3, 2))
        self.plus, self.minus = device(self.p), device(self.m)


def kernel(
    acts_hbm, pre_hbm, grad_hbm, w_in, w_out,
    o_ig, o_iw, o_ow, o_bias,
    acts, pre, grad, OUT,
    G, A, AC, D, WO, WI,
    HP, H1, H2, HX, HS, HB, ZR, SL,
    QP, Q1, Q2, QX, QS, ZS, ZL, IS, IR,
    ACC, WS, WR, BS, BR,
    send_sem, recv_sem, local_sem,
):
    gx, gy, gz = (lax.axis_index(name) for name in ("gx", "gy", "gz"))
    y, zl = gy // 2, lax.rem(gy, 2)
    zh, core = gz // 2, lax.rem(gz, 2)
    x = gx
    other = 1 - zl

    def dev(x_=x, y_=y, zl_=zl, zh_=zh, c_=core):
        return (x_, y_ * 2 + zl_, zh_ * 2 + c_)

    up, down, opp = (lax.rem(zh + k, 4) for k in (1, 3, 2))
    near = jnp.where(zl == 0, down, up)
    far = jnp.where(zl == 0, up, down)
    order = (zh, near, far, opp)
    ring = (zh, up, down, opp)
    twin = dev(c_=1 - core)
    pair = dev(zl_=other)
    rx = Ring(x, lambda k: dev(x_=k))
    ry = Ring(y, lambda k: dev(y_=k))

    peers = [rx.plus, rx.minus, ry.plus, ry.minus, twin, pair]
    peers += [dev(zh_=k) for k in (up, down, opp)]
    peers += [dev(zl_=other, zh_=near), dev(zl_=other, zh_=opp)]
    barrier = pltpu.get_barrier_semaphore()
    for peer in peers:
        pl.semaphore_signal(barrier, inc=1, device_id=peer, device_id_type=MESH)

    count = [0]
    sends = []

    def sem():
        count[0] += 1
        return count[0] - 1

    def send(k, src, dst, to):
        copy = pltpu.make_async_remote_copy(
            src_ref=src, dst_ref=dst, send_sem=send_sem.at[k], recv_sem=recv_sem.at[k],
            device_id=to, device_id_type=MESH,
        )
        copy.start()
        sends.append(copy)

    def arrived(k, dst):
        pltpu.make_async_remote_copy(
            src_ref=dst, dst_ref=dst, send_sem=send_sem.at[k], recv_sem=recv_sem.at[k],
            device_id=twin, device_id_type=MESH,
        ).wait_recv()

    n_local = [0]

    def local(src, dst):
        copy = pltpu.make_async_copy(src, dst, local_sem.at[n_local[0]])
        n_local[0] += 1
        copy.start()
        return copy

    staged = [local(a, b) for a, b in ((grad_hbm, grad), (pre_hbm, pre), (acts_hbm, acts))]

    def half(k):
        return pl.ds(pl.multiple_of(k * 32, 32), 32)

    LO, HI = pl.ds(0, 32), pl.ds(32, 32)

    class Rows:
        def __init__(self, src, buf):
            self.src, self.buf = src, buf
            self.k = [sem() for _ in range(6)]

        def columns(self, k):
            return self.src.at[:, pl.ds(pl.multiple_of(k * W, W), W)]

        def scatter(self):
            k, here = self.k, self.buf.at[zh, y, half(zl)]
            send(k[1], self.columns(far), here, dev(zh_=far))
            send(k[2], self.columns(near), here, dev(zl_=other, zh_=near))
            send(k[3], self.columns(opp), here, dev(zl_=other, zh_=opp))
            send(k[0], self.columns(zh), here, pair)
            self.own = local(self.columns(zh), here)

        def own_ready(self):
            self.own.wait()
            arrived(self.k[0], self.buf.at[zh, y, half(other)])

        def near_ready(self):
            block = self.buf.at[near, y]
            arrived(self.k[1], self.buf.at[near, y, half(zl)])
            arrived(self.k[2], self.buf.at[near, y, half(other)])
            send(self.k[4], block, block, pair)

        def far_ready(self):
            arrived(self.k[4], self.buf.at[far, y])

        def opp_half(self):
            piece = self.buf.at[opp, y, half(other)]
            arrived(self.k[3], piece)
            send(self.k[5], piece, piece, pair)

        def opp_ready(self):
            arrived(self.k[5], self.buf.at[opp, y, half(zl)])

    class Gather:
        def __init__(self, buf, ring, s):
            self.buf, self.ring, self.s = buf, ring, s
            self.k = [sem() for _ in range(4)]

        def at(self, block, rows=pl.ds(0, 64)):
            return self.buf.at[self.s, block, rows]

        def start(self):
            r, mine = self.ring, self.at(self.ring.me)
            send(self.k[0], mine, mine, r.plus)
            send(self.k[1], mine, mine, r.minus)

        def forward(self):
            r = self.ring
            arrived(self.k[0], self.at(r.m))
            send(self.k[2], self.at(r.m, LO), self.at(r.m, LO), r.plus)
            arrived(self.k[1], self.at(r.p))
            send(self.k[3], self.at(r.p, HI), self.at(r.p, HI), r.minus)

        def done(self):
            r = self.ring
            arrived(self.k[2], self.at(r.o, LO))
            arrived(self.k[3], self.at(r.o, HI))

    class Scatter:
        def __init__(self, part, first, second, mixed, ring, t):
            self.part, self.first, self.second, self.mixed = (
                part.at[t], first.at[t], second.at[t], mixed.at[t]
            )
            self.ring = ring
            self.k = [sem() for _ in range(6)]

        def start(self):
            r, k = self.ring, self.k
            send(k[0], self.part.at[r.o, LO], self.first.at[0], r.plus)
            send(k[1], self.part.at[r.o, HI], self.first.at[1], r.minus)
            send(k[2], self.part.at[r.p, HI], self.second.at[0, HI], r.plus)
            send(k[3], self.part.at[r.m, LO], self.second.at[1, LO], r.minus)

        def middle(self):
            r, k = self.ring, self.k
            for way, rows, block, to in ((0, LO, r.p, r.plus), (1, HI, r.m, r.minus)):
                arrived(k[way], self.first.at[way])
                total = self.part[block, rows].astype(F32) + self.first[way].astype(F32)
                self.mixed[way] = total.astype(BF)
                send(k[4 + way], self.mixed.at[way], self.second.at[way, rows], to)

        def end(self):
            k = self.k
            arrived(k[2], self.second.at[0, HI])
            arrived(k[3], self.second.at[1, LO])
            arrived(k[4], self.second.at[0, LO])
            arrived(k[5], self.second.at[1, HI])
            return (
                self.part[self.ring.me].astype(F32)
                + self.second[0].astype(F32)
                + self.second[1].astype(F32)
            )

    class Depth:
        def __init__(self, buf):
            self.buf = buf
            self.k = [sem() for _ in range(4)]

        def start(self):
            mine = self.buf.at[zh, x]
            send(self.k[0], mine, mine, dev(zh_=up))
            send(self.k[1], mine, mine, dev(zh_=down))

        def forward(self):
            for k, came, rows, to in ((0, down, LO, up), (1, up, HI, down)):
                arrived(self.k[k], self.buf.at[came, x])
                piece = self.buf.at[came, x, rows]
                send(self.k[k + 2], piece, piece, dev(zh_=to))

        def done(self):
            arrived(self.k[2], self.buf.at[opp, x, LO])
            arrived(self.k[3], self.buf.at[opp, x, HI])

    rows_g, rows_a = Rows(grad, G), Rows(acts, A)
    g_y = [Gather(G, ry, s) for s in order]
    a_y = [Gather(A, ry, s) for s in order]
    c_z, c_x = Depth(AC), [Gather(AC, rx, s) for s in order]
    h_x = [Scatter(HP, H1, H2, HX, rx, t) for t in range(4)]
    h_k = [sem() for _ in range(3)]
    d_z, d_x = Depth(D), [Gather(D, rx, s) for s in ring]
    q_y = [Scatter(QP, Q1, Q2, QX, ry, t) for t in range(4)]
    q_k = [sem() for _ in range(4)]
    i_k = [sem() for _ in range(3)]
    w_k = [sem() for _ in range(2)]
    g_k = [sem() for _ in range(2)]
    b_k = sem()
    OWN, NEAR, FAR, OPP = range(4)
    UP, DOWN = 1, 2

    mine = pl.ds(pl.multiple_of(core * 448, 448), 448)
    theirs = pl.ds(pl.multiple_of((1 - core) * 448, 448), 448)
    own_w = [None, None]
    results = []

    def weights(i, src, buf):
        send(w_k[i], src, buf.at[mine], twin)
        own_w[i] = local(src, buf.at[mine])

    def activations():
        staged[1].wait()
        value, slope = gelu_parts(pre[...].astype(F32))
        AC[zh, x] = value.astype(BF)
        SL[...] = slope

    def entry():
        pl.semaphore_wait(barrier, len(peers))
        staged[0].wait()

    def hidden(t, first=False):
        g_y[t].done()
        if first:
            own_w[0].wait()
            arrived(w_k[0], WO.at[theirs])
        part = dot(G[order[t]].reshape(256, W), WO[...], ((1,), (0,)))
        HP[t] = part.astype(BF).reshape(4, 64, W)
        h_x[t].start()

    def hidden_end(t):
        total = h_x[t].end()
        if t == OWN:
            HS[...] = total
        else:
            HB[t - 1] = total.astype(BF)
            send(h_k[t - 1], HB.at[t - 1], ZR.at[t - 1], dev(zh_=order[t]))

    def dh_rows():
        total = HS[...]
        for t in range(3):
            arrived(h_k[t], ZR.at[t])
            total = total + ZR[t].astype(F32)
        D[zh, x] = (total * SL[...]).astype(BF)

    def weight_grad(i, t, first=False):
        rows, cols = ((A, D), (G, AC))[i]
        s = ring[t] if i == 0 else order[t]
        right = cols[s].reshape(256, W)
        for low, size in ((0, 512), (512, 384)):
            left = rows[s, :, :, low : low + size].reshape(256, size)
            term = dot(left, right, ((0,), (0,)))
            if first:
                ACC[i, low : low + size] = term
            else:
                ACC[i, low : low + size] += term

    def share(i):
        WS[i] = ACC[i, theirs].astype(BF)
        send(g_k[i], WS.at[i], WR.at[i], twin)

    def inputs(t, first=False):
        d_x[t].done()
        if first:
            own_w[1].wait()
            arrived(w_k[1], WI.at[theirs])
        part = dot(D[ring[t]].reshape(256, W), WI[...], ((1,), (1,)))
        QP[t] = part.astype(BF).reshape(4, 64, W)
        q_y[t].start()

    def inputs_end(t):
        QS[t] = q_y[t].end()
        ZS[t] = QS[t, half(other)].astype(BF)
        send(q_k[t], ZS.at[t], ZL.at[t], pair)

    def inputs_out(t):
        arrived(q_k[t], ZL.at[t])
        total = (QS[t, half(zl)] + ZL[t].astype(F32)).astype(BF)
        if t == OWN:
            IR[zh] = total
        else:
            IS[t] = total
            send(i_k[t - 1], IS.at[t], IR.at[zh], dev(zh_=ring[t]))

    def bias_sums():
        BS[...] = jnp.sum(D[...].astype(F32).reshape(128, 8, W), axis=0)
        send(b_k, BS, BR, twin)

    def finish_bias():
        arrived(b_k, BR)
        o_bias[...] = jnp.sum(BS[...] + BR[...], axis=0, keepdims=True)

    def finish_weight(i, out):
        arrived(g_k[i], WR.at[i])
        OUT[i] = (ACC[i, mine] + WR[i].astype(F32)).astype(BF)
        results.append(local(OUT.at[i], out))

    def finish_inputs():
        for t in range(1, 4):
            arrived(i_k[(None, 1, 0, 2)[t]], IR.at[ring[t]])
        for k in range(4):
            results.append(local(IR.at[k], o_ig.at[:, pl.ds(k * W, W)]))

    def finish_sends():
        for copy in sends:
            copy.wait_send()
        for copy in results:
            copy.wait()

    activations()
    entry()
    rows_g.scatter()
    weights(0, w_out, WO)
    c_x[OWN].start()
    rows_g.near_ready()
    g_y[NEAR].start()
    rows_g.far_ready()
    g_y[FAR].start()
    rows_g.opp_half()
    g_y[NEAR].forward()
    rows_g.opp_ready()
    g_y[OPP].start()
    weights(1, w_in, WI)
    c_x[OWN].forward()
    g_y[FAR].forward()
    hidden(NEAR, True)
    rows_g.own_ready()
    g_y[OWN].start()
    g_y[OPP].forward()
    staged[2].wait()
    rows_a.scatter()
    h_x[NEAR].middle()
    hidden(FAR)
    g_y[OWN].forward()
    hidden_end(NEAR)
    h_x[FAR].middle()
    c_z.start()
    hidden(OPP)
    rows_a.near_ready()
    rows_a.opp_half()
    hidden_end(FAR)
    h_x[OPP].middle()
    rows_a.far_ready()
    a_y[NEAR].start()
    a_y[FAR].start()
    hidden(OWN)
    hidden_end(OPP)
    h_x[OWN].middle()
    rows_a.opp_ready()
    a_y[NEAR].forward()
    a_y[OPP].start()
    rows_a.own_ready()
    a_y[FAR].forward()
    a_y[OWN].start()
    hidden_end(OWN)
    c_z.forward()
    c_x[NEAR].start()
    c_x[OWN].done()
    weight_grad(1, OWN, True)
    dh_rows()
    d_x[OWN].start()
    d_z.start()
    c_x[NEAR].forward()
    a_y[OPP].forward()
    d_x[OWN].forward()
    a_y[OWN].forward()
    d_z.forward()
    d_x[UP].start()
    d_x[DOWN].start()
    inputs(OWN, True)
    q_y[OWN].middle()
    d_x[UP].forward()
    d_z.done()
    d_x[OPP].start()
    inputs_end(OWN)
    d_x[DOWN].forward()
    inputs(UP)
    inputs_out(OWN)
    c_x[FAR].start()
    q_y[UP].middle()
    for t in range(4):
        a_y[t].done()
    weight_grad(0, OWN, True)
    d_x[OPP].forward()
    inputs(DOWN)
    inputs_end(UP)
    q_y[DOWN].middle()
    c_x[FAR].forward()
    c_z.done()
    c_x[OPP].start()
    weight_grad(0, UP)
    inputs(OPP)
    inputs_end(DOWN)
    weight_grad(0, DOWN)
    inputs_out(UP)
    weight_grad(0, OPP)
    share(0)
    q_y[OPP].middle()
    inputs_out(DOWN)
    c_x[OPP].forward()
    c_x[NEAR].done()
    weight_grad(1, NEAR)
    c_x[FAR].done()
    weight_grad(1, FAR)
    inputs_end(OPP)
    bias_sums()
    finish_weight(0, o_iw)
    inputs_out(OPP)
    c_x[OPP].done()
    weight_grad(1, OPP)
    share(1)
    finish_bias()
    finish_inputs()
    finish_weight(1, o_ow)
    finish_sends()


def deliver(from_ig, from_iw, from_ow, from_bias, o_ig, o_iw, o_ow, o_bias, h_ig, h_iw, h_ow, get, put):
    pieces = []
    for src, held, dst, rows in (
        (from_iw, h_iw, o_iw, 224), (from_ow, h_ow, o_ow, 224), (from_ig, h_ig, o_ig, 32)
    ):
        for k in range(src.shape[0] // rows):
            at = pl.ds(k * rows, rows)
            pieces.append((src.at[at], held.at[at], dst.at[at]))
    ins = [pltpu.make_async_copy(a, b, get.at[k]) for k, (a, b, _) in enumerate(pieces)]
    outs = [pltpu.make_async_copy(b, c, put.at[k]) for k, (_, b, c) in enumerate(pieces)]
    for copy in ins:
        copy.start()
    o_bias[...] = from_bias[0]
    for came, go in zip(ins, outs):
        came.wait()
        go.start()
    for copy in outs:
        copy.wait()


def shards(acts, preact, out_grad, w_in, w_out):
    vmem = pl.BlockSpec(memory_space=pltpu.VMEM)
    bf = lambda *shape: pltpu.VMEM(shape, BF)
    f32 = lambda *shape: pltpu.VMEM(shape, F32)
    scratch = dict(
        acts=bf(32, 4 * W), pre=bf(64, W), grad=bf(32, 4 * W), OUT=bf(2, 448, W),
        G=bf(4, 4, 64, W), A=bf(4, 4, 64, W), AC=bf(4, 4, 64, W), D=bf(4, 4, 64, W),
        WO=bf(W, W), WI=bf(W, W),
        HP=bf(4, 4, 64, W), H1=bf(4, 2, 32, W), H2=bf(4, 2, 64, W), HX=bf(4, 2, 32, W),
        HS=f32(64, W), HB=bf(3, 64, W), ZR=bf(3, 64, W), SL=f32(64, W),
        QP=bf(4, 4, 64, W), Q1=bf(4, 2, 32, W), Q2=bf(4, 2, 64, W), QX=bf(4, 2, 32, W),
        QS=f32(4, 64, W), ZS=bf(4, 32, W), ZL=bf(4, 32, W), IS=bf(4, 32, W), IR=bf(4, 32, W),
        ACC=f32(2, W, W), WS=bf(2, 448, W), WR=bf(2, 448, W),
        BS=f32(8, W), BR=f32(8, W),
        send_sem=pltpu.SemaphoreType.DMA((N_SEMS,)),
        recv_sem=pltpu.SemaphoreType.DMA((N_SEMS,)),
        local_sem=pltpu.SemaphoreType.DMA((16,)),
    )
    hbm = pl.BlockSpec(memory_space=pl.ANY)
    parts = pl.pallas_call(
        kernel,
        out_shape=(
            jax.ShapeDtypeStruct((32, 4 * W), BF),
            jax.ShapeDtypeStruct((448, W), BF),
            jax.ShapeDtypeStruct((448, W), BF),
            jax.ShapeDtypeStruct((1, W), F32),
        ),
        in_specs=[hbm] * 5,
        out_specs=[hbm] * 3 + [vmem],
        scratch_shapes=list(scratch.values()),
        compiler_params=pltpu.CompilerParams(
            collective_id=0, has_side_effects=True, vmem_limit_bytes=60 * 2**20
        ),
    )(acts, preact, out_grad, w_in, w_out)
    return tuple(
        pl.pallas_call(
            deliver,
            out_shape=(
                jax.ShapeDtypeStruct((32, 4 * W), BF),
                jax.ShapeDtypeStruct((448, W), BF),
                jax.ShapeDtypeStruct((448, W), BF),
                jax.ShapeDtypeStruct((W,), F32),
            ),
            in_specs=[hbm] * 3 + [vmem],
            out_specs=[hbm] * 3 + [vmem],
            scratch_shapes=[
                bf(32, 4 * W), bf(448, W), bf(448, W),
                pltpu.SemaphoreType.DMA((5,)), pltpu.SemaphoreType.DMA((5,)),
            ],
        )(*parts)
    )


def solution(mesh):
    return jax.shard_map(
        shards,
        mesh=mesh,
        in_specs=(
            P(("gz", "gy"), "gx"),
            P(("gz", "gx"), "gy"),
            P(("gz", "gy"), "gx"),
            P(("gx", "gz"), "gy"),
            P(("gx", "gz"), "gy"),
        ),
        out_specs=(P(("gz", "gy"), "gx"), P(("gx", "gz"), "gy"), P(("gx", "gz"), "gy"), P("gy")),
        check_vma=False,
    )
```

time: 125 us -> 112 us (0.90)
  the two profiles are of different devices: /device:TPU:1 before, /device:TPU:32 now
where the time goes in v3:
time: 112 us; the launch traced here: 110 us
  Pallas kernels  109 us (97%)
    pallas_call x1, Pallas kernels, shards(): pl.pallas_call(kernel, out_shape=(jax.ShapeDtypeStruct((32, 4 * W), BF),...  106 us
    pallas_call x1, Pallas kernels, shards(): pl.pallas_call(deliver, out_shape=(jax.ShapeDtypeStruct((32, 4 * W), BF),...  3.55 us

profile of v3, /device:TPU:32, one launch (start us, length us, event | category | flops | bytes accessed | tf_op | source)
XLA Modules:
  0.0 110.0 jit_solution(9623850407645114197)
XLA Ops:
  0.6 105.8 %shard_map.84 = (bf16[32,3584]{1,0:T(8,128)(2,1)}, bf16[448,896]{1,0:T(8,128)(2,1)}, bf16[448,896]{1,0:T(8,128)(2,1)}, f32[1,896]{1,0:T(1,128)}) custom-call(bf16[32,3584]{1,0:T(8,128)(2,1)} %acts_hbm.1, bf16[64,896]{1,0:T(8,128)(2,1)} %pre_hbm.1, bf16[32,3584]{1,0:T(8,128)(2,1)} %grad_hbm.1, bf16[448,896]{1,0:T(8,128)(2,1)} %w_in.1, bf16[448,896]{1,0:T(8,128)(2,1)} %w_out.1), custom_call_target="tpu_custom_call" | custom-call | tf_op jit(solution)/shard_map/pallas_call | solution.py:496
  106.4 3.5 %shard_map.85 = (bf16[32,3584]{1,0:T(8,128)(2,1)}, bf16[448,896]{1,0:T(8,128)(2,1)}, bf16[448,896]{1,0:T(8,128)(2,1)}, f32[896]{0:T(1024)}) custom-call(bf16[32,3584]{1,0:T(8,128)(2,1)} %get-tuple-element.8.from_ig, bf16[448,896]{1,0:T(8,128)(2,1)} %get-tuple-element.9.from_iw, bf16[448,896]{1,0:T(8,128)(2,1)} %get-tuple-element.10.from_ow, ...), custom_call_target="tpu_custom_call" | custom-call | tf_op jit(solution)/shard_map/pallas_call | solution.py:512

commit v4 on v3

--- a/solution.py
+++ b/solution.py
@@ -37,7 +37,7 @@
 def kernel(
     acts_hbm, pre_hbm, grad_hbm, w_in, w_out,
     o_ig, o_iw, o_ow, o_bias,
-    acts, pre, grad, OUT,
+    acts, pre, grad,
     G, A, AC, D, WO, WI,
     HP, H1, H2, HX, HS, HB, ZR, SL,
     QP, Q1, Q2, QX, QS, ZS, ZL, IS, IR,
@@ -118,7 +118,11 @@
             k, here = self.k, self.buf.at[zh, y, half(zl)]
             send(k[1], self.columns(far), here, dev(zh_=far))
             send(k[2], self.columns(near), here, dev(zl_=other, zh_=near))
+
+        def scatter_rest(self):
+            k, here = self.k, self.buf.at[zh, y, half(zl)]
             send(k[3], self.columns(opp), here, dev(zl_=other, zh_=opp))
+            send(k[5], self.columns(opp), here, dev(zh_=opp))
             send(k[0], self.columns(zh), here, pair)
             self.own = local(self.columns(zh), here)
 
@@ -135,12 +139,8 @@
         def far_ready(self):
             arrived(self.k[4], self.buf.at[far, y])
 
-        def opp_half(self):
-            piece = self.buf.at[opp, y, half(other)]
-            arrived(self.k[3], piece)
-            send(self.k[5], piece, piece, pair)
-
         def opp_ready(self):
+            arrived(self.k[3], self.buf.at[opp, y, half(other)])
             arrived(self.k[5], self.buf.at[opp, y, half(zl)])
 
     class Gather:
@@ -242,7 +242,6 @@
     mine = pl.ds(pl.multiple_of(core * 448, 448), 448)
     theirs = pl.ds(pl.multiple_of((1 - core) * 448, 448), 448)
     own_w = [None, None]
-    results = []
 
     def weights(i, src, buf):
         send(w_k[i], src, buf.at[mine], twin)
@@ -327,24 +326,21 @@
 
     def finish_bias():
         arrived(b_k, BR)
-        o_bias[...] = jnp.sum(BS[...] + BR[...], axis=0, keepdims=True)
+        o_bias[...] = jnp.sum(BS[...] + BR[...], axis=0)
 
     def finish_weight(i, out):
         arrived(g_k[i], WR.at[i])
-        OUT[i] = (ACC[i, mine] + WR[i].astype(F32)).astype(BF)
-        results.append(local(OUT.at[i], out))
+        out[...] = (ACC[i, mine] + WR[i].astype(F32)).astype(BF)
 
     def finish_inputs():
         for t in range(1, 4):
             arrived(i_k[(None, 1, 0, 2)[t]], IR.at[ring[t]])
         for k in range(4):
-            results.append(local(IR.at[k], o_ig.at[:, pl.ds(k * W, W)]))
+            o_ig[:, k * W : (k + 1) * W] = IR[k]
 
     def finish_sends():
         for copy in sends:
             copy.wait_send()
-        for copy in results:
-            copy.wait()
 
     activations()
     entry()
@@ -353,125 +349,105 @@
     c_x[OWN].start()
     rows_g.near_ready()
     g_y[NEAR].start()
+    rows_g.scatter_rest()
+    g_y[NEAR].forward()
     rows_g.far_ready()
     g_y[FAR].start()
-    rows_g.opp_half()
-    g_y[NEAR].forward()
+    hidden(NEAR, True)
     rows_g.opp_ready()
     g_y[OPP].start()
-    weights(1, w_in, WI)
-    c_x[OWN].forward()
+    staged[2].wait()
+    rows_a.scatter()
+    rows_a.scatter_rest()
     g_y[FAR].forward()
-    hidden(NEAR, True)
     rows_g.own_ready()
     g_y[OWN].start()
     g_y[OPP].forward()
-    staged[2].wait()
-    rows_a.scatter()
+    hidden(FAR)
     h_x[NEAR].middle()
-    hidden(FAR)
     g_y[OWN].forward()
-    hidden_end(NEAR)
-    h_x[FAR].middle()
+    rows_a.near_ready()
+    c_x[OWN].forward()
     c_z.start()
     hidden(OPP)
-    rows_a.near_ready()
-    rows_a.opp_half()
-    hidden_end(FAR)
-    h_x[OPP].middle()
+    h_x[FAR].middle()
+    weights(1, w_in, WI)
+    hidden(OWN)
+    hidden_end(NEAR)
     rows_a.far_ready()
     a_y[NEAR].start()
+    h_x[OPP].middle()
+    c_z.forward()
+    rows_a.opp_ready()
     a_y[FAR].start()
-    hidden(OWN)
-    hidden_end(OPP)
+    hidden_end(FAR)
     h_x[OWN].middle()
-    rows_a.opp_ready()
     a_y[NEAR].forward()
     a_y[OPP].start()
+    hidden_end(OPP)
+    a_y[FAR].forward()
     rows_a.own_ready()
-    a_y[FAR].forward()
     a_y[OWN].start()
+    c_x[NEAR].start()
     hidden_end(OWN)
-    c_z.forward()
-    c_x[NEAR].start()
     c_x[OWN].done()
     weight_grad(1, OWN, True)
+    a_y[OPP].forward()
     dh_rows()
     d_x[OWN].start()
     d_z.start()
+    a_y[OWN].forward()
+    d_x[OWN].forward()
     c_x[NEAR].forward()
-    a_y[OPP].forward()
-    d_x[OWN].forward()
-    a_y[OWN].forward()
     d_z.forward()
     d_x[UP].start()
+    inputs(OWN, True)
+    for t in range(4):
+        a_y[t].done()
+    weight_grad(0, OWN, True)
     d_x[DOWN].start()
-    inputs(OWN, True)
-    q_y[OWN].middle()
     d_x[UP].forward()
     d_z.done()
     d_x[OPP].start()
-    inputs_end(OWN)
+    q_y[OWN].middle()
     d_x[DOWN].forward()
     inputs(UP)
-    inputs_out(OWN)
-    c_x[FAR].start()
-    q_y[UP].middle()
-    for t in range(4):
-        a_y[t].done()
-    weight_grad(0, OWN, True)
+    inputs_end(OWN)
     d_x[OPP].forward()
     inputs(DOWN)
+    q_y[UP].middle()
+    c_x[FAR].start()
+    inputs_out(OWN)
+    inputs(OPP)
+    q_y[DOWN].middle()
     inputs_end(UP)
-    q_y[DOWN].middle()
     c_x[FAR].forward()
     c_z.done()
     c_x[OPP].start()
     weight_grad(0, UP)
-    inputs(OPP)
+    q_y[OPP].middle()
     inputs_end(DOWN)
     weight_grad(0, DOWN)
     inputs_out(UP)
     weight_grad(0, OPP)
     share(0)
-    q_y[OPP].middle()
+    c_x[OPP].forward()
+    inputs_end(OPP)
     inputs_out(DOWN)
-    c_x[OPP].forward()
     c_x[NEAR].done()
     weight_grad(1, NEAR)
     c_x[FAR].done()
     weight_grad(1, FAR)
-    inputs_end(OPP)
-    bias_sums()
-    finish_weight(0, o_iw)
     inputs_out(OPP)
     c_x[OPP].done()
     weight_grad(1, OPP)
     share(1)
+    bias_sums()
+    finish_weight(0, o_iw)
     finish_bias()
+    finish_weight(1, o_ow)
     finish_inputs()
-    finish_weight(1, o_ow)
     finish_sends()
-
-
-def deliver(from_ig, from_iw, from_ow, from_bias, o_ig, o_iw, o_ow, o_bias, h_ig, h_iw, h_ow, get, put):
-    pieces = []
-    for src, held, dst, rows in (
-        (from_iw, h_iw, o_iw, 224), (from_ow, h_ow, o_ow, 224), (from_ig, h_ig, o_ig, 32)
-    ):
-        for k in range(src.shape[0] // rows):
-            at = pl.ds(k * rows, rows)
-            pieces.append((src.at[at], held.at[at], dst.at[at]))
-    ins = [pltpu.make_async_copy(a, b, get.at[k]) for k, (a, b, _) in enumerate(pieces)]
-    outs = [pltpu.make_async_copy(b, c, put.at[k]) for k, (_, b, c) in enumerate(pieces)]
-    for copy in ins:
-        copy.start()
-    o_bias[...] = from_bias[0]
-    for came, go in zip(ins, outs):
-        came.wait()
-        go.start()
-    for copy in outs:
-        copy.wait()
 
 
 def shards(acts, preact, out_grad, w_in, w_out):
@@ -479,7 +455,7 @@
     bf = lambda *shape: pltpu.VMEM(shape, BF)
     f32 = lambda *shape: pltpu.VMEM(shape, F32)
     scratch = dict(
-        acts=bf(32, 4 * W), pre=bf(64, W), grad=bf(32, 4 * W), OUT=bf(2, 448, W),
+        acts=bf(32, 4 * W), pre=bf(64, W), grad=bf(32, 4 * W),
         G=bf(4, 4, 64, W), A=bf(4, 4, 64, W), AC=bf(4, 4, 64, W), D=bf(4, 4, 64, W),
         WO=bf(W, W), WI=bf(W, W),
         HP=bf(4, 4, 64, W), H1=bf(4, 2, 32, W), H2=bf(4, 2, 64, W), HX=bf(4, 2, 32, W),
@@ -493,38 +469,16 @@
         local_sem=pltpu.SemaphoreType.DMA((16,)),
     )
     hbm = pl.BlockSpec(memory_space=pl.ANY)
-    parts = pl.pallas_call(
+    return pl.pallas_call(
         kernel,
-        out_shape=(
-            jax.ShapeDtypeStruct((32, 4 * W), BF),
-            jax.ShapeDtypeStruct((448, W), BF),
-            jax.ShapeDtypeStruct((448, W), BF),
-            jax.ShapeDtypeStruct((1, W), F32),
-        ),
+        out_shape=(bf(32, 4 * W), bf(448, W), bf(448, W), f32(W)),
         in_specs=[hbm] * 5,
-        out_specs=[hbm] * 3 + [vmem],
+        out_specs=[vmem] * 4,
         scratch_shapes=list(scratch.values()),
         compiler_params=pltpu.CompilerParams(
             collective_id=0, has_side_effects=True, vmem_limit_bytes=60 * 2**20
         ),
     )(acts, preact, out_grad, w_in, w_out)
-    return tuple(
-        pl.pallas_call(
-            deliver,
-            out_shape=(
-                jax.ShapeDtypeStruct((32, 4 * W), BF),
-                jax.ShapeDtypeStruct((448, W), BF),
-                jax.ShapeDtypeStruct((448, W), BF),
-                jax.ShapeDtypeStruct((W,), F32),
-            ),
-            in_specs=[hbm] * 3 + [vmem],
-            out_specs=[hbm] * 3 + [vmem],
-            scratch_shapes=[
-                bf(32, 4 * W), bf(448, W), bf(448, W),
-                pltpu.SemaphoreType.DMA((5,)), pltpu.SemaphoreType.DMA((5,)),
-            ],
-        )(*parts)
-    )
 
 
 def solution(mesh):

time: 112 us -> 100 us (0.89); the launches traced: 110 us -> 100 us
  Pallas kernels: 109 us -> 96.5 us
  local copies, waits for them, and re-layouts: 0 us -> 3.05 us
    pallas_call x2 -> x1, Pallas kernels: 109 us -> 96.5 us  [shards(): pl.pallas_call(kernel, out_shape=(bf(32, 4 * W), bf(448, W), bf(448, W),...]
    unnamed x0 -> x4, local copies, waits for them, and re-layouts: none -> 3.05 us
where the time goes in v4:
time: 100 us
  Pallas kernels  96.5 us (96%)
  local copies, waits for them, and re-layouts  3.05 us (3%)
    pallas_call x1, Pallas kernels, shards(): pl.pallas_call(kernel, out_shape=(bf(32, 4 * W), bf(448, W), bf(448, W),...  96.5 us
    unnamed x4, local copies, waits for them, and re-layouts  3.05 us

profile of v4, /device:TPU:32, one launch (start us, length us, event | category | flops | bytes accessed | tf_op | source)
XLA Modules:
  0.0 100.2 jit_solution(13393055961585161158)
XLA Ops:
  0.6 96.5 %shard_map.84 = (bf16[32,3584]{1,0:T(8,128)(2,1)S(1)}, bf16[448,896]{1,0:T(8,128)(2,1)S(1)}, bf16[448,896]{1,0:T(8,128)(2,1)S(1)}, f32[896]{0:T(1024)S(1)}) custom-call(bf16[32,3584]{1,0:T(8,128)(2,1)} %acts_hbm.1, bf16[64,896]{1,0:T(8,128)(2,1)} %pre_hbm.1, bf16[32,3584]{1,0:T(8,128)(2,1)} %grad_hbm.1, bf16[448,896]{1,0:T(8,128)(2,1)} %w_in.1, ...), custom_call_target="tpu_custom_call" | custom-call | tf_op jit(solution)/shard_map/pallas_call | solution.py:472
  97.1 0.7 copy.13
  97.8 0.6 copy.16
  98.4 0.9 copy.14
  99.3 0.9 copy.15

commit v5 on v4

--- a/solution.py
+++ b/solution.py
@@ -9,7 +9,8 @@
 BF = jnp.bfloat16
 F32 = jnp.float32
 W = 896
-N_SEMS = 160
+N_SEMS = 150
+N_SENDS = 40
 
 
 def gelu_parts(pre):
@@ -78,8 +79,11 @@
         return count[0] - 1
 
     def send(k, src, dst, to):
+        n = len(sends)
+        if n >= N_SENDS:
+            sends[n - N_SENDS].wait_send()
         copy = pltpu.make_async_remote_copy(
-            src_ref=src, dst_ref=dst, send_sem=send_sem.at[k], recv_sem=recv_sem.at[k],
+            src_ref=src, dst_ref=dst, send_sem=send_sem.at[n % N_SENDS], recv_sem=recv_sem.at[k],
             device_id=to, device_id_type=MESH,
         )
         copy.start()
@@ -87,7 +91,7 @@
 
     def arrived(k, dst):
         pltpu.make_async_remote_copy(
-            src_ref=dst, dst_ref=dst, send_sem=send_sem.at[k], recv_sem=recv_sem.at[k],
+            src_ref=dst, dst_ref=dst, send_sem=send_sem.at[0], recv_sem=recv_sem.at[k],
             device_id=twin, device_id_type=MESH,
         ).wait_recv()
 
@@ -118,13 +122,13 @@
             k, here = self.k, self.buf.at[zh, y, half(zl)]
             send(k[1], self.columns(far), here, dev(zh_=far))
             send(k[2], self.columns(near), here, dev(zl_=other, zh_=near))
+            send(k[0], self.columns(zh), here, pair)
+            self.own = local(self.columns(zh), here)
 
         def scatter_rest(self):
             k, here = self.k, self.buf.at[zh, y, half(zl)]
             send(k[3], self.columns(opp), here, dev(zl_=other, zh_=opp))
             send(k[5], self.columns(opp), here, dev(zh_=opp))
-            send(k[0], self.columns(zh), here, pair)
-            self.own = local(self.columns(zh), here)
 
         def own_ready(self):
             self.own.wait()
@@ -339,72 +343,71 @@
             o_ig[:, k * W : (k + 1) * W] = IR[k]
 
     def finish_sends():
-        for copy in sends:
+        for copy in sends[-N_SENDS:]:
             copy.wait_send()
 
     activations()
     entry()
     rows_g.scatter()
     weights(0, w_out, WO)
-    c_x[OWN].start()
     rows_g.near_ready()
     g_y[NEAR].start()
     rows_g.scatter_rest()
+    c_x[OWN].start()
+    rows_g.own_ready()
     g_y[NEAR].forward()
     rows_g.far_ready()
     g_y[FAR].start()
     hidden(NEAR, True)
     rows_g.opp_ready()
     g_y[OPP].start()
+    c_z.start()
+    g_y[FAR].forward()
+    g_y[OWN].start()
     staged[2].wait()
     rows_a.scatter()
     rows_a.scatter_rest()
-    g_y[FAR].forward()
-    rows_g.own_ready()
-    g_y[OWN].start()
+    h_x[NEAR].middle()
     g_y[OPP].forward()
     hidden(FAR)
-    h_x[NEAR].middle()
+    c_x[OWN].forward()
     g_y[OWN].forward()
+    hidden(OPP)
     rows_a.near_ready()
-    c_x[OWN].forward()
-    c_z.start()
-    hidden(OPP)
     h_x[FAR].middle()
-    weights(1, w_in, WI)
+    hidden_end(NEAR)
+    c_z.forward()
     hidden(OWN)
-    hidden_end(NEAR)
-    rows_a.far_ready()
+    h_x[OPP].middle()
     a_y[NEAR].start()
-    h_x[OPP].middle()
-    c_z.forward()
-    rows_a.opp_ready()
-    a_y[FAR].start()
     hidden_end(FAR)
     h_x[OWN].middle()
+    hidden_end(OPP)
+    weights(1, w_in, WI)
+    hidden_end(OWN)
+    c_x[NEAR].start()
+    rows_a.far_ready()
+    a_y[FAR].start()
+    rows_a.opp_ready()
     a_y[NEAR].forward()
     a_y[OPP].start()
-    hidden_end(OPP)
-    a_y[FAR].forward()
-    rows_a.own_ready()
-    a_y[OWN].start()
-    c_x[NEAR].start()
-    hidden_end(OWN)
     c_x[OWN].done()
     weight_grad(1, OWN, True)
-    a_y[OPP].forward()
+    c_x[FAR].start()
+    rows_a.own_ready()
     dh_rows()
     d_x[OWN].start()
     d_z.start()
-    a_y[OWN].forward()
+    a_y[FAR].forward()
+    a_y[OWN].start()
     d_x[OWN].forward()
     c_x[NEAR].forward()
+    c_x[FAR].forward()
+    a_y[OPP].forward()
     d_z.forward()
     d_x[UP].start()
     inputs(OWN, True)
-    for t in range(4):
-        a_y[t].done()
-    weight_grad(0, OWN, True)
+    a_y[OWN].forward()
     d_x[DOWN].start()
     d_x[UP].forward()
     d_z.done()
@@ -414,35 +417,36 @@
     inputs(UP)
     inputs_end(OWN)
     d_x[OPP].forward()
+    c_z.done()
+    c_x[OPP].start()
     inputs(DOWN)
     q_y[UP].middle()
-    c_x[FAR].start()
     inputs_out(OWN)
+    for t in range(4):
+        a_y[t].done()
+    weight_grad(0, OWN, True)
+    weight_grad(0, UP)
     inputs(OPP)
     q_y[DOWN].middle()
     inputs_end(UP)
-    c_x[FAR].forward()
-    c_z.done()
-    c_x[OPP].start()
-    weight_grad(0, UP)
-    q_y[OPP].middle()
-    inputs_end(DOWN)
     weight_grad(0, DOWN)
-    inputs_out(UP)
     weight_grad(0, OPP)
     share(0)
     c_x[OPP].forward()
-    inputs_end(OPP)
-    inputs_out(DOWN)
+    q_y[OPP].middle()
+    inputs_end(DOWN)
+    bias_sums()
     c_x[NEAR].done()
     weight_grad(1, NEAR)
+    inputs_end(OPP)
+    inputs_out(UP)
     c_x[FAR].done()
     weight_grad(1, FAR)
-    inputs_out(OPP)
+    inputs_out(DOWN)
     c_x[OPP].done()
     weight_grad(1, OPP)
     share(1)
-    bias_sums()
+    inputs_out(OPP)
     finish_weight(0, o_iw)
     finish_bias()
     finish_weight(1, o_ow)
@@ -464,7 +468,7 @@
         QS=f32(4, 64, W), ZS=bf(4, 32, W), ZL=bf(4, 32, W), IS=bf(4, 32, W), IR=bf(4, 32, W),
         ACC=f32(2, W, W), WS=bf(2, 448, W), WR=bf(2, 448, W),
         BS=f32(8, W), BR=f32(8, W),
-        send_sem=pltpu.SemaphoreType.DMA((N_SEMS,)),
+        send_sem=pltpu.SemaphoreType.DMA((N_SENDS,)),
         recv_sem=pltpu.SemaphoreType.DMA((N_SEMS,)),
         local_sem=pltpu.SemaphoreType.DMA((16,)),
     )

time: 100 us -> 94.8 us (0.948)
  Pallas kernels: 96.5 us -> 91 us
    pallas_call x1, Pallas kernels: 96.5 us -> 91 us  [shards(): pl.pallas_call(kernel, out_shape=(bf(32, 4 * W), bf(448, W), bf(448, W),...]
where the time goes in v5:
time: 94.8 us; the launch traced here: 94.7 us
  Pallas kernels  91 us (96%)
  local copies, waits for them, and re-layouts  3.05 us (3%)
    pallas_call x1, Pallas kernels, shards(): pl.pallas_call(kernel, out_shape=(bf(32, 4 * W), bf(448, W), bf(448, W),...  91 us
    unnamed x4, local copies, waits for them, and re-layouts  3.05 us

profile of v5, /device:TPU:32, one launch (start us, length us, event | category | flops | bytes accessed | tf_op | source)
XLA Modules:
  0.0 94.7 jit_solution(11679352267621105249)
XLA Ops:
  0.6 91.0 %shard_map.84 = (bf16[32,3584]{1,0:T(8,128)(2,1)S(1)}, bf16[448,896]{1,0:T(8,128)(2,1)S(1)}, bf16[448,896]{1,0:T(8,128)(2,1)S(1)}, f32[896]{0:T(1024)S(1)}) custom-call(bf16[32,3584]{1,0:T(8,128)(2,1)} %acts_hbm.1, bf16[64,896]{1,0:T(8,128)(2,1)} %pre_hbm.1, bf16[32,3584]{1,0:T(8,128)(2,1)} %grad_hbm.1, bf16[448,896]{1,0:T(8,128)(2,1)} %w_in.1, ...), custom_call_target="tpu_custom_call" | custom-call | tf_op jit(solution)/shard_map/pallas_call | solution.py:476
  91.7 0.7 copy.13
  92.4 0.6 copy.16
  93.0 0.9 copy.14
  93.9 0.9 copy.15

commit v6 on v5

--- a/solution.py
+++ b/solution.py
@@ -363,11 +363,11 @@
     g_y[OPP].start()
     c_z.start()
     g_y[FAR].forward()
-    g_y[OWN].start()
     staged[2].wait()
     rows_a.scatter()
     rows_a.scatter_rest()
     h_x[NEAR].middle()
+    g_y[OWN].start()
     g_y[OPP].forward()
     hidden(FAR)
     c_x[OWN].forward()
@@ -401,8 +401,6 @@
     a_y[FAR].forward()
     a_y[OWN].start()
     d_x[OWN].forward()
-    c_x[NEAR].forward()
-    c_x[FAR].forward()
     a_y[OPP].forward()
     d_z.forward()
     d_x[UP].start()
@@ -417,6 +415,8 @@
     inputs(UP)
     inputs_end(OWN)
     d_x[OPP].forward()
+    c_x[NEAR].forward()
+    c_x[FAR].forward()
     c_z.done()
     c_x[OPP].start()
     inputs(DOWN)
@@ -454,6 +454,19 @@
     finish_sends()
 
 
+def deliver(from_ig, from_iw, from_ow, from_bias, o_ig, o_iw, o_ow, o_bias, sem):
+    pieces = [(from_bias, o_bias)]
+    for src, dst, rows in ((from_iw, o_iw, 224), (from_ow, o_ow, 224), (from_ig, o_ig, 16)):
+        for k in range(src.shape[0] // rows):
+            at = pl.ds(k * rows, rows)
+            pieces.append((src.at[at], dst.at[at]))
+    copies = [pltpu.make_async_copy(a, b, sem.at[k]) for k, (a, b) in enumerate(pieces)]
+    for copy in copies:
+        copy.start()
+    for copy in copies:
+        copy.wait()
+
+
 def shards(acts, preact, out_grad, w_in, w_out):
     vmem = pl.BlockSpec(memory_space=pltpu.VMEM)
     bf = lambda *shape: pltpu.VMEM(shape, BF)
@@ -473,7 +486,7 @@
         local_sem=pltpu.SemaphoreType.DMA((16,)),
     )
     hbm = pl.BlockSpec(memory_space=pl.ANY)
-    return pl.pallas_call(
+    parts = pl.pallas_call(
         kernel,
         out_shape=(bf(32, 4 * W), bf(448, W), bf(448, W), f32(W)),
         in_specs=[hbm] * 5,
@@ -483,6 +496,14 @@
             collective_id=0, has_side_effects=True, vmem_limit_bytes=60 * 2**20
         ),
     )(acts, preact, out_grad, w_in, w_out)
+    return pl.pallas_call(
+        deliver,
+        out_shape=tuple(jax.ShapeDtypeStruct(p.shape, p.dtype) for p in parts),
+        in_specs=[vmem] * 4,
+        out_specs=[hbm] * 4,
+        scratch_shapes=[pltpu.SemaphoreType.DMA((7,))],
+        compiler_params=pltpu.CompilerParams(vmem_limit_bytes=2**20),
+    )(*parts)
 
 
 def solution(mesh):

time: 94.8 us -> 92.6 us (0.977)
  local copies, waits for them, and re-layouts: 3.05 us -> 0 us
    unnamed x4 -> x0, local copies, waits for them, and re-layouts: 3.05 us -> none
    pallas_call x0 -> x1, Pallas kernels: none -> 1.28 us  [shards(): pl.pallas_call(deliver, out_shape=tuple((jax.ShapeDtypeStruct(p.shape, p....]
where the time goes in v6:
time: 92.6 us; the launch traced here: 92.3 us
  Pallas kernels  91.6 us (99%)
    pallas_call x1, Pallas kernels, shards(): pl.pallas_call(kernel, out_shape=(bf(32, 4 * W), bf(448, W), bf(448, W),...  90.3 us

profile of v6, /device:TPU:32, one launch (start us, length us, event | category | flops | bytes accessed | tf_op | source)
XLA Modules:
  0.0 92.3 jit_solution(5906253332120298190)
XLA Ops:
  0.6 90.3 %shard_map.84 = (bf16[32,3584]{1,0:T(8,128)(2,1)S(1)}, bf16[448,896]{1,0:T(8,128)(2,1)S(1)}, bf16[448,896]{1,0:T(8,128)(2,1)S(1)}, f32[896]{0:T(1024)S(1)}) custom-call(bf16[32,3584]{1,0:T(8,128)(2,1)} %acts_hbm.1, bf16[64,896]{1,0:T(8,128)(2,1)} %pre_hbm.1, bf16[32,3584]{1,0:T(8,128)(2,1)} %grad_hbm.1, bf16[448,896]{1,0:T(8,128)(2,1)} %w_in.1, ...), custom_call_target="tpu_custom_call" | custom-call | tf_op jit(solution)/shard_map/pallas_call | solution.py:489
  91.0 1.3 %shard_map.85 = (bf16[32,3584]{1,0:T(8,128)(2,1)}, bf16[448,896]{1,0:T(8,128)(2,1)}, bf16[448,896]{1,0:T(8,128)(2,1)}, f32[896]{0:T(1024)}) custom-call(bf16[32,3584]{1,0:T(8,128)(2,1)S(1)} %get-tuple-element.8.from_ig, bf16[448,896]{1,0:T(8,128)(2,1)S(1)} %get-tuple-element.9.from_iw, bf16[448,896]{1,0:T(8,128)(2,1)S(1)} %get-tuple-element.10.from_ow, ...), custom_call_target="tpu_custom_call" | custom-call | tf_op jit(solution)/shard_map/pallas_call | solution.py:499

commit v7 on v6

--- a/solution.py
+++ b/solution.py
@@ -9,8 +9,8 @@
 BF = jnp.bfloat16
 F32 = jnp.float32
 W = 896
-N_SEMS = 150
-N_SENDS = 40
+N_SEMS = 100
+N_SENDS = 32
 
 
 def gelu_parts(pre):
@@ -113,7 +113,7 @@
     class Rows:
         def __init__(self, src, buf):
             self.src, self.buf = src, buf
-            self.k = [sem() for _ in range(6)]
+            self.k = [sem() for _ in range(4)]
 
         def columns(self, k):
             return self.src.at[:, pl.ds(pl.multiple_of(k * W, W), W)]
@@ -121,14 +121,14 @@
         def scatter(self):
             k, here = self.k, self.buf.at[zh, y, half(zl)]
             send(k[1], self.columns(far), here, dev(zh_=far))
-            send(k[2], self.columns(near), here, dev(zl_=other, zh_=near))
+            send(k[1], self.columns(near), here, dev(zl_=other, zh_=near))
             send(k[0], self.columns(zh), here, pair)
             self.own = local(self.columns(zh), here)
 
         def scatter_rest(self):
             k, here = self.k, self.buf.at[zh, y, half(zl)]
             send(k[3], self.columns(opp), here, dev(zl_=other, zh_=opp))
-            send(k[5], self.columns(opp), here, dev(zh_=opp))
+            send(k[3], self.columns(opp), here, dev(zh_=opp))
 
         def own_ready(self):
             self.own.wait()
@@ -136,21 +136,19 @@
 
         def near_ready(self):
             block = self.buf.at[near, y]
-            arrived(self.k[1], self.buf.at[near, y, half(zl)])
-            arrived(self.k[2], self.buf.at[near, y, half(other)])
-            send(self.k[4], block, block, pair)
+            arrived(self.k[1], block)
+            send(self.k[2], block, block, pair)
 
         def far_ready(self):
-            arrived(self.k[4], self.buf.at[far, y])
+            arrived(self.k[2], self.buf.at[far, y])
 
         def opp_ready(self):
-            arrived(self.k[3], self.buf.at[opp, y, half(other)])
-            arrived(self.k[5], self.buf.at[opp, y, half(zl)])
+            arrived(self.k[3], self.buf.at[opp, y])
 
     class Gather:
         def __init__(self, buf, ring, s):
             self.buf, self.ring, self.s = buf, ring, s
-            self.k = [sem() for _ in range(4)]
+            self.k = [sem() for _ in range(3)]
 
         def at(self, block, rows=pl.ds(0, 64)):
             return self.buf.at[self.s, block, rows]
@@ -165,12 +163,11 @@
             arrived(self.k[0], self.at(r.m))
             send(self.k[2], self.at(r.m, LO), self.at(r.m, LO), r.plus)
             arrived(self.k[1], self.at(r.p))
-            send(self.k[3], self.at(r.p, HI), self.at(r.p, HI), r.minus)
+            send(self.k[2], self.at(r.p, HI), self.at(r.p, HI), r.minus)
 
         def done(self):
             r = self.ring
-            arrived(self.k[2], self.at(r.o, LO))
-            arrived(self.k[3], self.at(r.o, HI))
+            arrived(self.k[2], self.at(r.o))
 
     class Scatter:
         def __init__(self, part, first, second, mixed, ring, t):
@@ -178,14 +175,14 @@
                 part.at[t], first.at[t], second.at[t], mixed.at[t]
             )
             self.ring = ring
-            self.k = [sem() for _ in range(6)]
+            self.k = [sem() for _ in range(3)]
 
         def start(self):
             r, k = self.ring, self.k
             send(k[0], self.part.at[r.o, LO], self.first.at[0], r.plus)
             send(k[1], self.part.at[r.o, HI], self.first.at[1], r.minus)
             send(k[2], self.part.at[r.p, HI], self.second.at[0, HI], r.plus)
-            send(k[3], self.part.at[r.m, LO], self.second.at[1, LO], r.minus)
+            send(k[2], self.part.at[r.m, LO], self.second.at[1, LO], r.minus)
 
         def middle(self):
             r, k = self.ring, self.k
@@ -193,14 +190,10 @@
                 arrived(k[way], self.first.at[way])
                 total = self.part[block, rows].astype(F32) + self.first[way].astype(F32)
                 self.mixed[way] = total.astype(BF)
-                send(k[4 + way], self.mixed.at[way], self.second.at[way, rows], to)
+                send(k[2], self.mixed.at[way], self.second.at[way, rows], to)
 
         def end(self):
-            k = self.k
-            arrived(k[2], self.second.at[0, HI])
-            arrived(k[3], self.second.at[1, LO])
-            arrived(k[4], self.second.at[0, LO])
-            arrived(k[5], self.second.at[1, HI])
+            arrived(self.k[2], self.second)
             return (
                 self.part[self.ring.me].astype(F32)
                 + self.second[0].astype(F32)
@@ -210,29 +203,31 @@
     class Depth:
         def __init__(self, buf):
             self.buf = buf
-            self.k = [sem() for _ in range(4)]
+            self.k = [sem() for _ in range(3)]
 
         def start(self):
             mine = self.buf.at[zh, x]
             send(self.k[0], mine, mine, dev(zh_=up))
             send(self.k[1], mine, mine, dev(zh_=down))
 
-        def forward(self):
-            for k, came, rows, to in ((0, down, LO, up), (1, up, HI, down)):
-                arrived(self.k[k], self.buf.at[came, x])
+        def here(self):
+            arrived(self.k[0], self.buf.at[down, x])
+            arrived(self.k[1], self.buf.at[up, x])
+
+        def send_on(self):
+            for came, rows, to in ((down, LO, up), (up, HI, down)):
                 piece = self.buf.at[came, x, rows]
-                send(self.k[k + 2], piece, piece, dev(zh_=to))
+                send(self.k[2], piece, piece, dev(zh_=to))
 
         def done(self):
-            arrived(self.k[2], self.buf.at[opp, x, LO])
-            arrived(self.k[3], self.buf.at[opp, x, HI])
+            arrived(self.k[2], self.buf.at[opp, x])
 
     rows_g, rows_a = Rows(grad, G), Rows(acts, A)
     g_y = [Gather(G, ry, s) for s in order]
     a_y = [Gather(A, ry, s) for s in order]
     c_z, c_x = Depth(AC), [Gather(AC, rx, s) for s in order]
     h_x = [Scatter(HP, H1, H2, HX, rx, t) for t in range(4)]
-    h_k = [sem() for _ in range(3)]
+    h_k = sem()
     d_z, d_x = Depth(D), [Gather(D, rx, s) for s in ring]
     q_y = [Scatter(QP, Q1, Q2, QX, ry, t) for t in range(4)]
     q_k = [sem() for _ in range(4)]
@@ -276,12 +271,12 @@
             HS[...] = total
         else:
             HB[t - 1] = total.astype(BF)
-            send(h_k[t - 1], HB.at[t - 1], ZR.at[t - 1], dev(zh_=order[t]))
+            send(h_k, HB.at[t - 1], ZR.at[t - 1], dev(zh_=order[t]))
 
     def dh_rows():
         total = HS[...]
+        arrived(h_k, ZR)
         for t in range(3):
-            arrived(h_k[t], ZR.at[t])
             total = total + ZR[t].astype(F32)
         D[zh, x] = (total * SL[...]).astype(BF)
 
@@ -376,7 +371,6 @@
     rows_a.near_ready()
     h_x[FAR].middle()
     hidden_end(NEAR)
-    c_z.forward()
     hidden(OWN)
     h_x[OPP].middle()
     a_y[NEAR].start()
@@ -385,6 +379,7 @@
     hidden_end(OPP)
     weights(1, w_in, WI)
     hidden_end(OWN)
+    c_z.here()
     c_x[NEAR].start()
     rows_a.far_ready()
     a_y[FAR].start()
@@ -402,11 +397,13 @@
     a_y[OWN].start()
     d_x[OWN].forward()
     a_y[OPP].forward()
-    d_z.forward()
+    d_z.here()
     d_x[UP].start()
+    d_z.send_on()
     inputs(OWN, True)
     a_y[OWN].forward()
     d_x[DOWN].start()
+    c_z.send_on()
     d_x[UP].forward()
     d_z.done()
     d_x[OPP].start()
@@ -432,10 +429,10 @@
     weight_grad(0, DOWN)
     weight_grad(0, OPP)
     share(0)
-    c_x[OPP].forward()
     q_y[OPP].middle()
     inputs_end(DOWN)
     bias_sums()
+    c_x[OPP].forward()
     c_x[NEAR].done()
     weight_grad(1, NEAR)
     inputs_end(OPP)

time: 92.6 us -> 92 us (level)
  no operation moved by 1% of the time
where the time goes in v7:
time: 92 us; the launch traced here: 91.5 us
  Pallas kernels  90.9 us (99%)
    pallas_call x1, Pallas kernels, shards(): pl.pallas_call(kernel, out_shape=(bf(32, 4 * W), bf(448, W), bf(448, W),...  89.6 us

profile of v7, /device:TPU:32, one launch (start us, length us, event | category | flops | bytes accessed | tf_op | source)
XLA Modules:
  0.0 91.5 jit_solution(7497933717423179385)
XLA Ops:
  0.6 89.6 %shard_map.84 = (bf16[32,3584]{1,0:T(8,128)(2,1)S(1)}, bf16[448,896]{1,0:T(8,128)(2,1)S(1)}, bf16[448,896]{1,0:T(8,128)(2,1)S(1)}, f32[896]{0:T(1024)S(1)}) custom-call(bf16[32,3584]{1,0:T(8,128)(2,1)} %acts_hbm.1, bf16[64,896]{1,0:T(8,128)(2,1)} %pre_hbm.1, bf16[32,3584]{1,0:T(8,128)(2,1)} %grad_hbm.1, bf16[448,896]{1,0:T(8,128)(2,1)} %w_in.1, ...), custom_call_target="tpu_custom_call" | custom-call | tf_op jit(solution)/shard_map/pallas_call | solution.py:486
  90.2 1.3 %shard_map.85 = (bf16[32,3584]{1,0:T(8,128)(2,1)}, bf16[448,896]{1,0:T(8,128)(2,1)}, bf16[448,896]{1,0:T(8,128)(2,1)}, f32[896]{0:T(1024)}) custom-call(bf16[32,3584]{1,0:T(8,128)(2,1)S(1)} %get-tuple-element.8.from_ig, bf16[448,896]{1,0:T(8,128)(2,1)S(1)} %get-tuple-element.9.from_iw, bf16[448,896]{1,0:T(8,128)(2,1)S(1)} %get-tuple-element.10.from_ow, ...), custom_call_target="tpu_custom_call" | custom-call | tf_op jit(solution)/shard_map/pallas_call | solution.py:496

commit v8 on v7

--- a/solution.py
+++ b/solution.py
@@ -426,23 +426,23 @@
     inputs(OPP)
     q_y[DOWN].middle()
     inputs_end(UP)
+    c_x[OPP].forward()
     weight_grad(0, DOWN)
     weight_grad(0, OPP)
     share(0)
     q_y[OPP].middle()
     inputs_end(DOWN)
     bias_sums()
-    c_x[OPP].forward()
     c_x[NEAR].done()
     weight_grad(1, NEAR)
-    inputs_end(OPP)
-    inputs_out(UP)
     c_x[FAR].done()
     weight_grad(1, FAR)
-    inputs_out(DOWN)
     c_x[OPP].done()
     weight_grad(1, OPP)
     share(1)
+    inputs_end(OPP)
+    inputs_out(UP)
+    inputs_out(DOWN)
     inputs_out(OPP)
     finish_weight(0, o_iw)
     finish_bias()

time: 92 us -> 92.2 us (level)
  no operation moved by 1% of the time
where the time goes in v8:
time: 92.2 us; the launch traced here: 92.1 us
  Pallas kernels  91.5 us (99%)
    pallas_call x1, Pallas kernels, shards(): pl.pallas_call(kernel, out_shape=(bf(32, 4 * W), bf(448, W), bf(448, W),...  90.2 us

profile of v8, /device:TPU:32, one launch (start us, length us, event | category | flops | bytes accessed | tf_op | source)
XLA Modules:
  0.0 92.1 jit_solution(16490359983491702568)
XLA Ops:
  0.6 90.2 %shard_map.84 = (bf16[32,3584]{1,0:T(8,128)(2,1)S(1)}, bf16[448,896]{1,0:T(8,128)(2,1)S(1)}, bf16[448,896]{1,0:T(8,128)(2,1)S(1)}, f32[896]{0:T(1024)S(1)}) custom-call(bf16[32,3584]{1,0:T(8,128)(2,1)} %acts_hbm.1, bf16[64,896]{1,0:T(8,128)(2,1)} %pre_hbm.1, bf16[32,3584]{1,0:T(8,128)(2,1)} %grad_hbm.1, bf16[448,896]{1,0:T(8,128)(2,1)} %w_in.1, ...), custom_call_target="tpu_custom_call" | custom-call | tf_op jit(solution)/shard_map/pallas_call | solution.py:486
  90.8 1.3 %shard_map.85 = (bf16[32,3584]{1,0:T(8,128)(2,1)}, bf16[448,896]{1,0:T(8,128)(2,1)}, bf16[448,896]{1,0:T(8,128)(2,1)}, f32[896]{0:T(1024)}) custom-call(bf16[32,3584]{1,0:T(8,128)(2,1)S(1)} %get-tuple-element.8.from_ig, bf16[448,896]{1,0:T(8,128)(2,1)S(1)} %get-tuple-element.9.from_iw, bf16[448,896]{1,0:T(8,128)(2,1)S(1)} %get-tuple-element.10.from_ow, ...), custom_call_target="tpu_custom_call" | custom-call | tf_op jit(solution)/shard_map/pallas_call | solution.py:496

commit v9 on v7

--- a/solution.py
+++ b/solution.py
@@ -341,10 +341,10 @@
         for copy in sends[-N_SENDS:]:
             copy.wait_send()
 
-    activations()
     entry()
     rows_g.scatter()
     weights(0, w_out, WO)
+    activations()
     rows_g.near_ready()
     g_y[NEAR].start()
     rows_g.scatter_rest()

time: 92 us -> 92.1 us (level)
  no operation moved by 1% of the time
where the time goes in v9:
time: 92.1 us; the launch traced here: 91.6 us
  Pallas kernels  91 us (99%)
    pallas_call x1, Pallas kernels, shards(): pl.pallas_call(kernel, out_shape=(bf(32, 4 * W), bf(448, W), bf(448, W),...  89.7 us

profile of v9, /device:TPU:32, one launch (start us, length us, event | category | flops | bytes accessed | tf_op | source)
XLA Modules:
  0.0 91.6 jit_solution(18266899430079142635)
XLA Ops:
  0.6 89.7 %shard_map.84 = (bf16[32,3584]{1,0:T(8,128)(2,1)S(1)}, bf16[448,896]{1,0:T(8,128)(2,1)S(1)}, bf16[448,896]{1,0:T(8,128)(2,1)S(1)}, f32[896]{0:T(1024)S(1)}) custom-call(bf16[32,3584]{1,0:T(8,128)(2,1)} %acts_hbm.1, bf16[64,896]{1,0:T(8,128)(2,1)} %pre_hbm.1, bf16[32,3584]{1,0:T(8,128)(2,1)} %grad_hbm.1, bf16[448,896]{1,0:T(8,128)(2,1)} %w_in.1, ...), custom_call_target="tpu_custom_call" | custom-call | tf_op jit(solution)/shard_map/pallas_call | solution.py:486
  90.3 1.3 %shard_map.85 = (bf16[32,3584]{1,0:T(8,128)(2,1)}, bf16[448,896]{1,0:T(8,128)(2,1)}, bf16[448,896]{1,0:T(8,128)(2,1)}, f32[896]{0:T(1024)}) custom-call(bf16[32,3584]{1,0:T(8,128)(2,1)S(1)} %get-tuple-element.8.from_ig, bf16[448,896]{1,0:T(8,128)(2,1)S(1)} %get-tuple-element.9.from_iw, bf16[448,896]{1,0:T(8,128)(2,1)S(1)} %get-tuple-element.10.from_ow, ...), custom_call_target="tpu_custom_call" | custom-call | tf_op jit(solution)/shard_map/pallas_call | solution.py:496
